TPU v7x, 32 devices: a whole 2x2x4 slice. The times are simulated.
32 devices in a mesh: row: 4 (over z), col: 8 (over y, x, core).
Axes of the slice: x: 2, y: 2, z: 4, core: 2. Of those that a mesh axis runs over, the one named last changes fastest.
Arguments:
- src_emb: bfloat16 [32768, 256], P(('row', 'col')), may hold values from -64 to 64
- dst_emb: bfloat16 [32768, 256], P('col'), may hold values from -64 to 64
- state_emb: bfloat16 [32768, 256], P('col'), may hold values from -64 to 64
- word_emb: bfloat16 [32000, 256], P('row'), may hold values from -64 to 64
- start_probs: bfloat16 [64, 32768], P(None, 'row'), may hold values from 0.099609375 to 10
- token_ids: int32 [64, 2], replicated, may hold values from 0 to 31999
Outputs:
- final_probs: float32 [64, 32768], P(None, 'col')
- log_norm: float32 [64], replicated
All inputs are finite; a program needn't handle non-finite values.
Results may differ from a plain program's by a relative error of at most 0.0003.
The roundings to bfloat16 on the way count: a program that leaves them out, or rounds other values in their place, can miss the bound.
Values may be sent and summed in bfloat16 or wider, within the bound.
No kernel may reach another device: no remote copies, remote signals or barrier semaphores. Data moves between devices by JAX's collectives and lax.ppermute only.
A program may use at most 256 MiB of HBM per device.

v0:
```python
import jax
import jax.numpy as jnp
from jax import lax
from jax.sharding import PartitionSpec as P

S = 32768


def merged(shard, axis, combine):
    everything = jax.tree.map(lambda part: lax.all_gather(part, axis), shard)
    first = jax.tree.map(lambda part: part[0], everything)

    def step(k, so_far):
        return combine(so_far, jax.tree.map(lambda part: part[k], everything))

    return lax.fori_loop(1, lax.axis_size(axis), step, first)


def merge_stats(first, second):
    top = jnp.maximum(first[0], second[0])
    return (top, first[1] * jnp.exp(first[0] - top) + second[1] * jnp.exp(second[0] - top))


def on_device(src_emb, dst_emb, state_emb, word_emb, start_probs, token_ids):
    src_rows = lax.all_gather(src_emb, "col", axis=0, tiled=True)
    logits = jnp.dot(src_rows, dst_emb.T, preferred_element_type=jnp.float32)
    local_top = jnp.max(logits, axis=1)
    local_total = jnp.sum(jnp.exp(logits - local_top[:, None]), axis=1)
    row_top, row_total = merged((local_top, local_total), "col", merge_stats)
    shifted = jnp.exp(logits - row_top[:, None])
    trans = shifted.astype(jnp.bfloat16)
    vocab_rows = word_emb.shape[0]
    vocab_logits = jnp.dot(state_emb, word_emb.T, preferred_element_type=jnp.float32)
    vocab_top = jnp.max(vocab_logits, axis=1)
    vocab_total = jnp.sum(jnp.exp(vocab_logits - vocab_top[:, None]), axis=1)
    vocab_top, vocab_total = merged((vocab_top, vocab_total), "row", merge_stats)
    state_norm = vocab_top + jnp.log(vocab_total)
    row_id = lax.axis_index("row")
    flat_ids = token_ids.reshape(-1) - row_id * vocab_rows
    onehot = (flat_ids[:, None] == jnp.arange(vocab_rows, dtype=jnp.int32)[None, :]).astype(
        jnp.bfloat16
    )
    picked = jnp.dot(onehot, word_emb, preferred_element_type=jnp.float32)
    token_vecs = lax.psum(picked.astype(jnp.bfloat16), "row")
    batch = token_ids.shape[0]
    count_steps = token_ids.shape[1]
    dest_count = state_emb.shape[0]
    scores = jnp.dot(token_vecs, state_emb.T, preferred_element_type=jnp.float32)
    emit = jnp.exp(scores - state_norm[None, :]).reshape(batch, count_steps, dest_count)
    source_count = src_rows.shape[0]
    weights0 = (start_probs.astype(jnp.float32) / row_total[None, :]).astype(jnp.bfloat16)
    partial_value = jnp.dot(weights0, trans, preferred_element_type=jnp.float32)
    summed = lax.psum(partial_value, "row")
    joint1 = summed * emit[:, 0]
    scale1 = lax.psum(jnp.sum(joint1, axis=1), "col") / S
    probs1 = (joint1 / scale1[:, None]).astype(jnp.bfloat16)
    gathered = lax.all_gather(probs1, "col", axis=1, tiled=True)
    source_probs = lax.dynamic_slice_in_dim(gathered, row_id * source_count, source_count, 1)
    weights1 = (source_probs.astype(jnp.float32) / row_total[None, :]).astype(jnp.bfloat16)
    partial2 = jnp.dot(weights1, trans, preferred_element_type=jnp.float32)
    summed2 = lax.psum(partial2, "row")
    joint2 = summed2 * emit[:, 1]
    scale2 = lax.psum(jnp.sum(joint2, axis=1), "col") / S
    final_probs = joint2 / scale2[:, None]
    log_norm = jnp.log(scale1) + jnp.log(scale2)
    return (final_probs, log_norm)


def solution(mesh):
    in_specs = (
        P(("row", "col"), None),
        P("col", None),
        P("col", None),
        P("row", None),
        P(None, "row"),
        P(),
    )
    out_specs = (P(None, "col"), P())
    return jax.shard_map(
        on_device, mesh=mesh, in_specs=in_specs, out_specs=out_specs, check_vma=False
    )
```

profile of v0, /device:TPU:0, one launch (start us, length us, event | category | flops | bytes accessed | tf_op | source)
XLA Modules:
  0.0 517.5 jit_solution(6087537097404258977)
XLA Ops:
  8.0 0.0 all-gather.7.cloned.1.call-start
  8.1 0.7 all-gather.7.cloned.1.call-update
  8.7 0.0 all-reduce.6.cloned.1.call-start
  8.8 0.7 broadcast_subtract_fusion
  9.5 0.1 copy.12
  9.6 0.1 sub.91
  9.7 3.5 fusion.5
  13.3 0.0 all-reduce.6.cloned.1.call-update
  13.3 0.0 all-reduce.4.cloned.1.call-start
  13.3 48.2 %fusion.16 = (f32[4096]{0:T(1024)S(1)}, f32[4096,8000]{0,1:T(8,128)}) fusion(bf16[4096,256]{1,0:T(8,128)(2,1)} %param.12, bf16[8000,256]{1,0:T(8,128)(2,1)} %param.13), kind=kOutput, calls=%fused_computation.38 | convolution fusion | flops 16809979904 | bytes 137281536 | tf_op jit(solution)/shard_map/dot_general | solution.py:33
  61.5 40.3 %exponential_reduce_fusion.1 = f32[4096]{0:T(1024)S(1)} fusion(f32[4096,8000]{0,1:T(8,128)} %get-tuple-element.307, f32[4096]{0:T(1024)S(1)} %get-tuple-element.306), kind=kLoop, calls=%fused_computation.8 | loop fusion | flops 65531904 | bytes 131104768 | tf_op jit(solution)/shard_map/reduce_sum | solution.py:35
  101.8 14.6 %all-gather.3 = f32[16384]{0:T(1024)S(1)} all-gather(f32[4096]{0:T(1024)S(1)} %exponential_reduce_fusion.1), channel_id=5, replica_groups=mesh['row'=4,'col'=8] {'row'}, dimensions={0}, use_global_device_ids=true | all-gather | bytes 81920 | tf_op jit(solution)/shard_map/all_gather | solution.py:10
  116.4 13.2 %all-gather.2 = f32[16384]{0:T(1024)S(1)} all-gather(f32[4096]{0:T(1024)S(1)} %get-tuple-element.306), channel_id=4, replica_groups=mesh['row'=4,'col'=8] {'row'}, dimensions={0}, use_global_device_ids=true | all-gather | bytes 81920 | tf_op jit(solution)/shard_map/all_gather | solution.py:10
  129.6 0.3 while.35
  129.9 0.0 all-gather.7.cloned.1.call-done
  130.0 47.1 %fusion.15 = (f32[8192]{0:T(1024)S(1)}, f32[8192,4096]{0,1:T(8,128)}) fusion(bf16[8192,256]{1,0:T(8,128)(2,1)} %all-gather.7.cloned.1.call-done, bf16[4096,256]{1,0:T(8,128)(2,1)S(1)} %copy-done), kind=kOutput, calls=%fused_computation.37 | convolution fusion | flops 17213415424 | bytes 140541952 | tf_op jit(solution)/shard_map/dot_general | solution.py:26
  177.1 40.8 %exponential_reduce_fusion = f32[8192]{0:T(1024)S(1)} fusion(f32[8192,4096]{0,1:T(8,128)} %get-tuple-element.305, f32[8192]{0:T(1024)S(1)} %get-tuple-element.304), kind=kLoop, calls=%fused_computation.7 | loop fusion | flops 67100672 | bytes 134283264 | tf_op jit(solution)/shard_map/reduce_sum | solution.py:28
  217.9 9.5 %all-gather.1 = f32[65536]{0:T(1024)S(1)} all-gather(f32[8192]{0:T(1024)S(1)} %exponential_reduce_fusion), channel_id=3, replica_groups=mesh['row'=4,'col'=8] {'col'}, dimensions={0}, use_global_device_ids=true | all-gather | bytes 294912 | tf_op jit(solution)/shard_map/all_gather | solution.py:10
  227.4 0.7 reshape.24
  228.1 9.6 %all-gather = f32[65536]{0:T(1024)S(1)} all-gather(f32[8192]{0:T(1024)S(1)} %get-tuple-element.304), channel_id=2, replica_groups=mesh['row'=4,'col'=8] {'col'}, dimensions={0}, use_global_device_ids=true | all-gather | bytes 294912 | tf_op jit(solution)/shard_map/all_gather | solution.py:10
  237.7 0.8 reshape.23
  238.5 8.0 %while.34 = (s32[]{:T(128)}, f32[8192]{0:T(1024)S(1)}, f32[8192]{0:T(1024)S(1)}, f32[8,8192]{1,0:T(8,128)}, f32[8,8192]{1,0:T(8,128)}, /*index=5*/s32[]{:T(128)}, s32[]{:T(128)}, s32[]{:T(128)}) while((s32[]{:T(128)}, f32[8192]{0:T(1024)S(1)}, f32[8192]{0:T(1024)S(1)}, f32[8,8192]{1,0:T(8,128)}, f32[8,8192]{1,0:T(8,128)}, ...), condition=%wide.region_3.0_spmd, body=%wide.region_2.0_spmd.sunk | while | flops 49157 | bytes 327811 | solution.py:16
  238.5 1.1 constant_dynamic-slice_fusion.6
  239.6 1.1 constant_dynamic-slice_fusion.6
  240.8 1.1 constant_dynamic-slice_fusion.6
  241.9 1.1 constant_dynamic-slice_fusion.6
  243.1 1.1 constant_dynamic-slice_fusion.6
  244.2 1.1 constant_dynamic-slice_fusion.6
  245.4 1.1 constant_dynamic-slice_fusion.6
  246.5 43.9 %fusion.1 = f32[64,4096]{1,0:T(8,128)} fusion(f32[8192,4096]{0,1:T(8,128)} %get-tuple-element.305, f32[8192]{0:T(1024)S(1)} %get-tuple-element.269, bf16[64,8192]{1,0:T(8,128)(2,1)S(1)} %copy-done.1, f32[8192]{0:T(1024)S(1)} %get-tuple-element.268), kind=kOutput, calls=%fused_computation.10 | convolution fusion | flops 4363649024 | bytes 136380416 | tf_op jit(solution)/shard_map/dot_general | solution.py:52
  290.4 0.0 all-reduce.4.cloned.1.call-update
  290.4 0.0 all-gather.9.cloned.1.call-start
  290.4 0.0 all-reduce.6.cloned.1.call-done
  290.5 3.8 fusion.2
  294.3 3.5 reshape.22
  297.7 5.4 %fusion.14 = (f32[64,1,4096]{2,1,0:T(1,128)S(1)}, f32[64,1,4096]{2,1,0:T(1,128)}) fusion(f32[64,2,4096]{2,1,0:T(2,128)} %reshape.22), kind=kLoop, calls=%fused_computation.36 | loop fusion | bytes 4194304 | tf_op jit(solution)/shard_map/slice | solution.py:62
  303.2 39.0 %all-reduce.4.cloned.1.call-done = f32[64,4096]{1,0:T(8,128)} async-done(((f32[64,4096]{1,0:T(8,128)}), f32[64,4096]{1,0:T(8,128)}) %all-reduce.4.cloned.1.call-update) | async-done | bytes 1048592 | tf_op jit(solution)/shard_map/psum | solution.py:53
  342.1 2.3 fusion.11
  344.4 13.3 %psum.37 = f32[64]{0:T(128)S(1)} all-reduce(f32[64]{0:T(128)S(1)} %fusion.11), channel_id=1, replica_groups=mesh['row'=4,'col'=8] {'col'}, use_global_device_ids=true, to_apply=%region_11.0 | all-reduce | flops 64 | bytes 512 | tf_op jit(solution)/shard_map/psum | solution.py:55
  357.7 3.0 divide_convert_fusion.4
  360.7 0.0 all-reduce.8.cloned.1.call-start
  360.8 34.8 %all-gather.9.cloned.1.call-done = bf16[64,32768]{1,0:T(8,128)(2,1)} async-done(((bf16[64,4096]{1,0:T(8,128)(2,1)}), bf16[64,32768]{1,0:T(8,128)(2,1)}) %all-gather.9.cloned.1.call-update) | async-done | bytes 4194320 | tf_op jit(solution)/shard_map/all_gather | solution.py:57
  395.5 43.8 %fusion = f32[64,4096]{1,0:T(8,128)} fusion(f32[8192,4096]{0,1:T(8,128)} %get-tuple-element.305, f32[8192]{0:T(1024)S(1)} %get-tuple-element.269, bf16[64,32768]{1,0:T(8,128)(2,1)} %all-gather.9.cloned.1.call-done, s32[]{:T(128)S(6)} %select_n.25, f32[8192]{0:T(1024)S(1)} %get-tuple-element.268), kind=kOutput, calls=%fused_computation.9 | convolution fusion | flops 4363649024 | bytes 136380416 | tf_op jit(solution)/shard_map/dot_general | solution.py:60
  439.4 51.9 %all-reduce.8.cloned.1.call-done = f32[64,4096]{1,0:T(8,128)} async-done(((f32[64,4096]{1,0:T(8,128)}), f32[64,4096]{1,0:T(8,128)}) %all-reduce.8.cloned.1.call-update) | async-done | bytes 1048592 | tf_op jit(solution)/shard_map/psum | solution.py:61
  491.2 1.9 fusion.12
  493.2 13.3 %psum.39 = f32[64]{0:T(128)S(1)} all-reduce(f32[64]{0:T(128)S(1)} %fusion.12), channel_id=1, replica_groups=mesh['row'=4,'col'=8] {'col'}, use_global_device_ids=true, to_apply=%region_14.0 | all-reduce | flops 64 | bytes 512 | tf_op jit(solution)/shard_map/psum | solution.py:63
  506.5 0.5 log_add_fusion.1
  507.0 2.9 broadcast_divide_fusion
  (27 shorter events, 0.6 us)
Async XLA Ops:
  8.0 122.0 %copy-start = (bf16[4096,256]{1,0:T(8,128)(2,1)S(1)}, bf16[4096,256]{1,0:T(8,128)(2,1)}, u32[]{:S(2)}) copy-start(bf16[4096,256]{1,0:T(8,128)(2,1)} %param.11) | copy-start | bytes 6291460
  8.0 121.9 %all-gather.7.cloned.1.call-start = ((), (), s32[]{:S(2)}) async-start(), calls=%async_computation | async-start | bytes 4718592 | tf_op jit(solution)/shard_map/all_gather | solution.py:25
  8.7 281.7 %all-reduce.6.cloned.1.call-start = ((), (), s32[]{:S(2)}) async-start(), calls=%async_computation.2 | async-start | bytes 131072 | tf_op jit(solution)/shard_map/psum | solution.py:44
  13.3 328.8 %all-reduce.4.cloned.1.call-start = ((), (), s32[]{:S(2)}) async-start(), calls=%async_computation.1 | async-start | bytes 2097152 | tf_op jit(solution)/shard_map/psum | solution.py:53
  217.9 28.6 %copy-start.1 = (bf16[64,8192]{1,0:T(8,128)(2,1)S(1)}, bf16[64,8192]{1,0:T(8,128)(2,1)}, u32[]{:S(2)}) copy-start(bf16[64,8192]{1,0:T(8,128)(2,1)} %param.14) | copy-start | bytes 3145732
  290.4 105.1 %all-gather.9.cloned.1.call-start = ((), (), s32[]{:S(2)}) async-start(), calls=%async_computation.3 | async-start | bytes 4718592 | tf_op jit(solution)/shard_map/all_gather | solution.py:57
  360.7 130.5 %all-reduce.8.cloned.1.call-start = ((), (), s32[]{:S(2)}) async-start(), calls=%async_computation.4 | async-start | bytes 2097152 | tf_op jit(solution)/shard_map/psum | solution.py:61
Sparse Core Ops, SparseCore 0:
  10.9 39.4 all-gather.6
  360.8 34.6 all-gather.8
Sparse Core Ops, SparseCore 1:
  13.4 36.5 all-reduce.5
  290.5 51.6 all-reduce.3
  439.4 51.7 all-reduce.7
where the time goes:
time: 518 us
  matrix products  190 us (37%)
  waiting for transfers between devices  126 us (24%)
  other arithmetic  92.8 us (18%)
  blocking collectives  73.5 us (14%)
  local copies, waits for them, and re-layouts  18.4 us (4%)
  between operations  15.8 us (3%)
    psum x1, waiting for transfers between devices, on_device(): summed2 = lax.psum(partial2, 'row')  51.9 us
    dot_general x1, matrix products, on_device(): jnp.dot(state_emb, word_emb.T, preferred_element_type=jnp.float32)  48.2 us
    dot_general x1, matrix products, on_device(): logits = jnp.dot(src_rows, dst_emb.T, preferred_element_type=jnp.float32)  47.1 us
    all_gather x4, blocking collectives, merged(): everything = jax.tree.map(lambda part: lax.all_gather(part, axis), shard)  46.8 us
    dot_general x1, matrix products, on_device(): partial_value = jnp.dot(weights0, trans, preferred_element_type=jnp.float32)  43.9 us
    dot_general x1, matrix products, on_device(): partial2 = jnp.dot(weights1, trans, preferred_element_type=jnp.float32)  43.8 us
    reduce_sum x1, other arithmetic, on_device(): local_total = jnp.sum(jnp.exp(logits - local_top[:, None]), axis=1)  40.8 us
    reduce_sum x1, other arithmetic, on_device(): vocab_total = jnp.sum(jnp.exp(vocab_logits - vocab_top[:, None]), axis=1)  40.3 us
  transfers between devices with their start and end apart: 5, of which 3 were waited for; matrix products, arithmetic and copies ran while one was open for 48% of the time, Pallas kernels for 0%

commit v1 on v0

v1 whole, which is shorter than its diff:
```python
import functools

import jax
import jax.numpy as jnp
from jax import lax
from jax.experimental import pallas as pl
from jax.experimental.pallas import tpu as pltpu
from jax.sharding import PartitionSpec as P

F32 = jnp.float32
BF16 = jnp.bfloat16
NT = (((1,), (1,)), ((), ()))
SPREAD = 60.0
VMEM_LIMIT = 48 * 1024 * 1024


def block_of(count, most):
    return max(size for size in range(16, most + 1, 16) if count % size == 0)


def params():
    return pltpu.CompilerParams(
        vmem_limit_bytes=VMEM_LIMIT, dimension_semantics=("arbitrary",)
    )


def logits_of(rows, columns):
    return lax.dot_general(rows, columns, NT, preferred_element_type=F32)


def stats_kernel(x_ref, y_ref, top_ref, total_ref, buf0, buf1, *, rows, sub):
    count, columns = x_ref.shape[0], y_ref.shape[0]
    bufs = (buf0, buf1)
    head = min(rows, 256)
    units = [(c, a) for c in range(0, columns, sub) for a in range(0, count, rows)]

    def multiply(unit, buf):
        c, a = unit
        logits = logits_of(x_ref[a : a + rows, :], y_ref[c : c + sub, :])
        buf[...] = logits
        top = jnp.max(logits.reshape(rows // 8, 8, sub), axis=0)
        shift = jnp.max(logits[:head], axis=0, keepdims=True) if a == 0 else None
        return top, shift

    worst = jnp.zeros((1, sub), F32)
    upcoming = multiply(units[0], buf0)
    top = total = shift = None
    for k, (c, a) in enumerate(units):
        unit_top, unit_shift = upcoming
        if a == 0:
            shift, top = unit_shift, unit_top
        else:
            top = jnp.maximum(top, unit_top)
        if k + 1 < len(units):
            upcoming = multiply(units[k + 1], bufs[(k + 1) % 2])
        part = jnp.sum(jnp.exp(bufs[k % 2][...] - shift).reshape(rows // 8, 8, sub), axis=0)
        total = part if a == 0 else total + part
        if a + rows == count:
            total = jnp.sum(total, axis=0, keepdims=True)
            top = jnp.max(top, axis=0, keepdims=True)
            worst = jnp.maximum(worst, top - shift)
            top_ref[:, c : c + sub] = top
            total_ref[:, c : c + sub] = total / jnp.exp(top - shift)

    @pl.when(jnp.max(worst) > SPREAD)
    def again():
        for c in range(0, columns, sub):

            def logits_at(k):
                part = x_ref[pl.ds(pl.multiple_of(k * rows, rows), rows), :]
                return logits_of(part, y_ref[c : c + sub, :])

            def max_step(k, so_far):
                return jnp.maximum(so_far, jnp.max(logits_at(k), axis=0, keepdims=True))

            top = lax.fori_loop(0, count // rows, max_step, jnp.full((1, sub), -jnp.inf, F32))

            def sum_step(k, so_far):
                return so_far + jnp.sum(jnp.exp(logits_at(k) - top), axis=0, keepdims=True)

            total = lax.fori_loop(0, count // rows, sum_step, jnp.zeros((1, sub), F32))
            top_ref[:, c : c + sub] = top
            total_ref[:, c : c + sub] = total


def column_stats(x, y, name):
    count, depth = x.shape
    columns = y.shape[0]
    width = block_of(columns, 1024)
    sub = block_of(width, 256)
    rows = block_of(count, 1024)
    return pl.pallas_call(
        functools.partial(stats_kernel, rows=rows, sub=sub),
        grid=(columns // width,),
        in_specs=[
            pl.BlockSpec((count, depth), lambda i: (0, 0)),
            pl.BlockSpec((width, depth), lambda i: (i, 0)),
        ],
        out_specs=[pl.BlockSpec((1, width), lambda i: (0, i))] * 2,
        out_shape=[jax.ShapeDtypeStruct((1, columns), F32)] * 2,
        scratch_shapes=[pltpu.VMEM((rows, sub), F32)] * 2,
        compiler_params=params(),
        cost_estimate=pl.CostEstimate(
            flops=2 * count * columns * depth,
            bytes_accessed=2 * depth * (count + columns),
            transcendentals=count * columns,
        ),
        name=name,
    )(x, y)


def trans_kernel(src_ref, dst_ref, top_ref, weight_ref, trans_ref, out_ref, buf0, buf1, *, cols):
    count = dst_ref.shape[0] // cols
    bufs = (buf0, buf1)

    @pl.when(pl.program_id(0) == 0)
    def _():
        out_ref[...] = jnp.zeros_like(out_ref)

    def multiply(k):
        bufs[k % 2][...] = logits_of(src_ref[...], dst_ref[k * cols : (k + 1) * cols, :])

    def advance(k):
        here = slice(k * cols, (k + 1) * cols)
        out_ref[:, here] += jnp.dot(
            weight_ref[...], trans_ref[:, here], preferred_element_type=F32
        )

    multiply(0)
    for k in range(count):
        if k + 1 < count:
            multiply(k + 1)
        shifted = jnp.exp(bufs[k % 2][...] - top_ref[...])
        trans_ref[:, k * cols : (k + 1) * cols] = shifted.astype(BF16)
        if k > 0:
            advance(k - 1)
    advance(count - 1)


def build_and_advance(src, dst, top, weights):
    sources, depth = src.shape
    dests = dst.shape[0]
    batch = weights.shape[0]
    rows = block_of(sources, 1024)
    cols = block_of(dests, 256)
    return pl.pallas_call(
        functools.partial(trans_kernel, cols=cols),
        grid=(sources // rows,),
        in_specs=[
            pl.BlockSpec((rows, depth), lambda i: (i, 0)),
            pl.BlockSpec((dests, depth), lambda i: (0, 0)),
            pl.BlockSpec((rows, 1), lambda i: (i, 0)),
            pl.BlockSpec((batch, rows), lambda i: (0, i)),
        ],
        out_specs=[
            pl.BlockSpec((rows, dests), lambda i: (i, 0)),
            pl.BlockSpec((batch, dests), lambda i: (0, 0)),
        ],
        out_shape=[
            jax.ShapeDtypeStruct((sources, dests), BF16),
            jax.ShapeDtypeStruct((batch, dests), F32),
        ],
        scratch_shapes=[pltpu.VMEM((rows, cols), F32)] * 2,
        compiler_params=params(),
        cost_estimate=pl.CostEstimate(
            flops=2 * sources * dests * (depth + batch),
            bytes_accessed=2 * sources * dests,
            transcendentals=sources * dests,
        ),
        name="build_trans",
    )(src, dst, top, weights)


def advance_kernel(weight_ref, trans_ref, out_ref):
    @pl.when(pl.program_id(0) == 0)
    def _():
        out_ref[...] = jnp.zeros_like(out_ref)

    out_ref[...] += jnp.dot(weight_ref[...], trans_ref[...], preferred_element_type=F32)


def advance(weights, trans):
    sources, dests = trans.shape
    batch = weights.shape[0]
    rows = block_of(sources, 2048)
    return pl.pallas_call(
        advance_kernel,
        grid=(sources // rows,),
        in_specs=[
            pl.BlockSpec((batch, rows), lambda i: (0, i)),
            pl.BlockSpec((rows, dests), lambda i: (i, 0)),
        ],
        out_specs=pl.BlockSpec((batch, dests), lambda i: (0, 0)),
        out_shape=jax.ShapeDtypeStruct((batch, dests), F32),
        compiler_params=params(),
        cost_estimate=pl.CostEstimate(
            flops=2 * sources * dests * batch,
            bytes_accessed=2 * sources * dests,
            transcendentals=0,
        ),
        name="advance",
    )(weights, trans)


def bits_of(count):
    return [1 << k for k in range(count.bit_length() - 1)]


def swapped(value, axis, mask):
    count = lax.axis_size(axis)
    return lax.ppermute(value, axis, [(i, i ^ mask) for i in range(count)])


def summed_all(value, axes):
    for axis in axes:
        for mask in bits_of(lax.axis_size(axis)):
            value = value + swapped(value, axis, mask)
    return value


def merged_rows(stats, rows):
    others = [swapped(stats, "row", mask) for mask in range(1, rows)]
    top = functools.reduce(jnp.maximum, [part[0] for part in others], stats[0])
    totals = [part[1] * jnp.exp(part[0] - top) for part in [stats] + others]
    while len(totals) > 1:
        totals = [first + second for first, second in zip(totals[::2], totals[1::2])]
    return top, totals[0]


def tied(value, others):
    return lax.optimization_barrier((value, *others))[0]


def widths_of(dests):
    unit = block_of(dests, 256)
    count = dests // unit
    last = max(1, count // 8)
    rest = count - last
    first = [rest // 3 + (k < rest % 3) for k in range(3)]
    return [unit * size for size in first + [last] if size]


def add(value, received):
    return value + received


def root_hops(rows, cols):
    per_row = cols // rows
    hops = []
    for hop in range(1, rows):
        perm = []
        for col in range(cols):
            root = col // per_row
            if hop <= root:
                perm.append(((hop - 1) * cols + col, hop * cols + col))
            if hop <= rows - 1 - root:
                perm.append(((rows - hop) * cols + col, (rows - hop - 1) * cols + col))
        hops.append((lambda value, perm=perm: lax.ppermute(value, ("row", "col"), perm), add))
    return hops


def everywhere_hops(middle):
    return [
        (lambda value: lax.ppermute(value, "row", [(0, 1), (3, 2)]), add),
        (lambda value: lax.ppermute(value, "row", [(1, 2), (2, 1)]), add),
        (
            lambda value: lax.ppermute(value, "row", [(1, 0), (2, 3)]),
            lambda value, received: jnp.where(middle, value, received),
        ),
    ]


def piped(compute, operand, count, hops, small, rounds):
    moving, ready = [], []
    for k in range(count):
        part = compute(k, tied(operand, ready) if ready else operand)
        received = [hops[at][0](value) if at < len(hops) else value for value, at in moving]
        part, *received = lax.optimization_barrier((part, *received))
        moving = [
            (hops[at][1](value, got), at + 1) if at < len(hops) else (value, at)
            for (value, at), got in zip(moving, received)
        ]
        ready = [value for value, at in moving]
        moving.append((part, 0))
    small = small()
    for k in range(len(hops)):
        received = [hops[at][0](value) if at < len(hops) else value for value, at in moving]
        for step in rounds[k]:
            small = step(small)
        small, *received = lax.optimization_barrier((small, *received))
        moving = [
            (hops[at][1](value, got), at + 1) if at < len(hops) else (value, at)
            for (value, at), got in zip(moving, received)
        ]
    return [value for value, at in moving], small


def to_sources(block, rows, cols):
    per_row = cols // rows
    row, col = lax.axis_index("row"), lax.axis_index("col")
    group = col // per_row
    relation = group ^ row
    half = block.shape[1] // 2
    first, second = block[:, :half], block[:, half:]

    def sent(value, pairs):
        at = lambda r, mask, m: r * cols + (r ^ mask) * per_row + m
        perm = [
            (at(r, a, m), at(r, b, m)) for r in range(rows) for a, b in pairs for m in range(per_row)
        ]
        return lax.ppermute(value, ("row", "col"), perm)

    first = jnp.where(relation == 0, first, sent(first, [(0, 1)]))
    second = jnp.where(relation == 0, second, sent(second, [(0, 2)]))
    first = jnp.where(relation <= 1, first, sent(first, [(0, 2), (1, 3)]))
    second = jnp.where((relation == 0) | (relation == 2), second, sent(second, [(0, 1), (2, 3)]))
    blocks = jnp.concatenate([first, second], axis=1)
    member = col % per_row
    for mask in bits_of(per_row):
        other = swapped(blocks, "col", mask)
        blocks = jnp.where(
            member & mask == 0,
            jnp.concatenate([blocks, other], axis=1),
            jnp.concatenate([other, blocks], axis=1),
        )
    return blocks


def on_device(src_emb, dst_emb, state_emb, word_emb, start_probs, token_ids):
    rows, cols = lax.axis_size("row"), lax.axis_size("col")
    row = lax.axis_index("row")
    middle = (row == 1) | (row == 2)
    batch, steps = token_ids.shape
    dests = dst_emb.shape[0]
    states = dests * cols

    src_rows = lax.all_gather(src_emb, "col", axis=0, tiled=True)

    vocab = jnp.stack(column_stats(word_emb, state_emb, "vocab_stats"))
    vocab_top, vocab_total = merged_rows(vocab, rows)
    state_norm = vocab_top + jnp.log(vocab_total)

    vocab_rows = word_emb.shape[0]
    flat_ids = token_ids.T.reshape(-1) - row * vocab_rows
    onehot = (flat_ids[:, None] == jnp.arange(vocab_rows, dtype=jnp.int32)[None, :]).astype(BF16)
    picked = jnp.dot(onehot, word_emb, preferred_element_type=F32).astype(BF16)
    token_vecs = summed_all(picked, ("row",))
    scores = logits_of(token_vecs, state_emb)
    emit = jnp.exp(scores - state_norm)

    stats = jnp.stack(column_stats(dst_emb, src_rows, "trans_stats"))
    every = lax.all_gather(stats, "col")
    row_top = jnp.max(every[:, 0], axis=0)
    row_total = jnp.sum(every[:, 1] * jnp.exp(every[:, 0] - row_top[None]), axis=0)

    weights0 = (start_probs.astype(F32) / row_total).astype(BF16)
    top_column = row_top.reshape(-1, 1)
    widths = widths_of(dests)
    starts = [sum(widths[:k]) for k in range(len(widths))]
    here = [slice(at, at + width) for at, width in zip(starts, widths)]

    trans, scales1 = [], []

    def add_over(axis, mask):
        return lambda value: value + swapped(value, axis, mask)

    def add_rows(value):
        if rows != 4:
            return summed_all(value, ("row",))
        one, two, three = [swapped(value, "row", mask) for mask in (1, 2, 3)]
        return (value + one) + (two + three)

    col_rounds = [add_over("col", mask) for mask in bits_of(cols)]

    def first_step(k, weights):
        built, part = build_and_advance(src_rows, dst_emb[here[k]], top_column, weights)
        trans.append(built)
        scales1.append(jnp.sum(part * emit[:batch, here[k]], axis=1))
        return part

    sums1, scale1 = piped(
        first_step,
        weights0,
        len(widths),
        root_hops(rows, cols),
        lambda: sum(scales1),
        [col_rounds, [add_rows], []],
    )
    scale1 = scale1 / states
    joint1 = jnp.concatenate(sums1, axis=1) * emit[:batch]
    probs1 = (joint1 / scale1[:, None]).astype(BF16)
    source_probs = to_sources(probs1, rows, cols)
    weights1 = (source_probs.astype(F32) / row_total).astype(BF16)

    def second_step(k, weights):
        return advance(weights, trans[k])

    sums2, _ = piped(
        second_step,
        weights1,
        len(widths),
        everywhere_hops(middle),
        lambda: scale1,
        [[], [], []],
    )
    joint2 = jnp.concatenate(sums2, axis=1) * emit[batch : 2 * batch]
    scale2 = summed_all(jnp.sum(joint2, axis=1), ("col",)) / states
    final_probs = joint2 / scale2[:, None]
    log_norm = jnp.log(scale1) + jnp.log(scale2)
    return (final_probs, log_norm)


def solution(mesh):
    in_specs = (
        P(("row", "col"), None),
        P("col", None),
        P("col", None),
        P("row", None),
        P(None, "row"),
        P(),
    )
    out_specs = (P(None, "col"), P())
    return jax.shard_map(
        on_device, mesh=mesh, in_specs=in_specs, out_specs=out_specs, check_vma=False
    )
```

time: 518 us -> 393 us (0.76)
  matrix products: 190 us -> 5.26 us
  Pallas kernels: 0 us -> 171 us
  other arithmetic: 92.8 us -> 13 us
  starting transfers between devices: 0.21 us -> 78.2 us
  waiting for transfers between devices: 126 us -> 69.3 us
  blocking collectives: 73.5 us -> 33.4 us
  local copies, waits for them, and re-layouts: 18.4 us -> 10.4 us
    dot_general x6 -> x2, matrix products: 190 us -> 5.26 us  [the longest x1 3.07 us: on_device(): picked = jnp.dot(onehot, word_emb, preferred_element_type=F32).astype(BF16)]
    pallas_call x0 -> x10, Pallas kernels: none -> 171 us  [the longest x2 89.9 us: column_stats(): pl.pallas_call(functools.partial(stats_kernel, rows=rows, sub=sub), grid=...]
    psum x3 -> x0, waiting for transfers between devices: 90.9 us -> none  [the longest x1 51.9 us: on_device(): summed2 = lax.psum(partial2, 'row')]
    reduce_sum x4 -> x5, other arithmetic: 85.3 us -> 1.08 us  [the longest x1 0.47 us: on_device(): jnp.sum(every[:, 1] * jnp.exp(every[:, 0] - row_top[None]), axis=0)]
    ppermute x0 -> x43, starting transfers between devices: none -> 78.2 us  [the longest x15 30.8 us: swapped(): return lax.ppermute(value, axis, [(i, i ^ mask) for i in range(count)])]
    ppermute x0 -> x43, waiting for transfers between devices: none -> 68.6 us  [the longest x12 28.7 us: root_hops(): lax.ppermute(value, ('row', 'col'), perm)]
    all_gather x1 -> x0, waiting for transfers between devices: 34.8 us -> none  [on_device(): gathered = lax.all_gather(probs1, 'col', axis=1, tiled=True)]
    psum x2 -> x0, blocking collectives: 26.6 us -> none  [the longest x1 13.3 us: on_device(): scale1 = lax.psum(jnp.sum(joint1, axis=1), 'col') / S]
  transfers between devices with their start and end apart: 5 -> 44, of which waited for: 3 -> 20; matrix products, arithmetic and copies ran while one was open for 48% -> 3% of each run, Pallas kernels for 0% -> 28%
where the time goes in v1:
time: 393 us; the launch traced here: 395 us
  Pallas kernels  171 us (44%)
  starting transfers between devices  78.2 us (20%)
  waiting for transfers between devices  69.3 us (18%)
  blocking collectives  33.4 us (8%)
  between operations  14.7 us (4%)
  other arithmetic  13 us (3%)
  local copies, waits for them, and re-layouts  10.4 us (3%)
  matrix products  5.26 us (1%)
    pallas_call x2, Pallas kernels, column_stats(): pl.pallas_call(functools.partial(stats_kernel, rows=rows, sub=sub), grid=...  89.9 us
    pallas_call x4, Pallas kernels, build_and_advance(): pl.pallas_call(functools.partial(trans_kernel, cols=cols), grid=(sources...  50.8 us
    all_gather x1, blocking collectives, on_device(): every = lax.all_gather(stats, 'col')  33.4 us
    ppermute x15, starting transfers between devices, swapped(): return lax.ppermute(value, axis, [(i, i ^ mask) for i in range(count)])  30.8 us
    pallas_call x4, Pallas kernels, advance(): pl.pallas_call(advance_kernel, grid=(sources // rows,), in_specs=[pl.Bloc...  30.5 us
    ppermute x12, waiting for transfers between devices, root_hops(): lax.ppermute(value, ('row', 'col'), perm)  28.7 us
    ppermute x4, starting transfers between devices, everywhere_hops(): lax.ppermute(value, 'row', [(0, 1), (3, 2)])  20.7 us
    ppermute x15, waiting for transfers between devices, swapped(): return lax.ppermute(value, axis, [(i, i ^ mask) for i in range(count)])  16.6 us
  transfers between devices with their start and end apart: 44, of which 20 were waited for; matrix products, arithmetic and copies ran while one was open for 3% of the time, Pallas kernels for 28%

profile of v1, /device:TPU:0, one launch (start us, length us, event | category | flops | bytes accessed | tf_op | source)
XLA Modules:
  0.0 395.4 jit_solution(1595454239823938207)
XLA Ops:
  7.9 1.6 copy-done
  9.5 2.2 copy-done.6
  11.7 50.8 %vocab_stats.1 = (f32[1,4096]{1,0:T(1,128)S(1)}, f32[1,4096]{1,0:T(1,128)S(1)}) custom-call(bf16[8000,256]{1,0:T(8,128)(2,1)S(1)} %copy-done.6, bf16[4096,256]{1,0:T(8,128)(2,1)S(1)} %copy-done), custom_call_target="tpu_custom_call" | custom-call | flops 16777216000 | bytes 6193152 | tf_op jit(solution)/shard_map/vocab_stats/pallas_call | solution.py:92
  62.5 5.1 %collective-permute-start.10 = (f32[2,1,4096]{2,1,0:T(1,128)S(1)}, f32[2,1,4096]{2,1,0:T(1,128)S(1)}, u32[]{:S(2)}, u32[]{:S(2)}) collective-permute-start(f32[2,1,4096]{2,1,0:T(1,128)S(1)} %pad_maximum_fusion.2), channel_id=1, source_target_pairs={{0,24},{8,16},{16,8},{24,0},{1,25},{9,17},{17,9},{25,1},{2,26},{10... | collective-permute-start | bytes 98312 | tf_op jit(solution)/shard_map/ppermute | solution.py:211
  68.3 3.1 fusion.3
  71.4 1.5 collective-permute-start.6
  75.8 2.4 collective-permute-start.7
  79.0 2.0 collective-permute-done.7
  81.0 2.2 fusion
  83.2 39.1 %trans_stats.1 = (f32[1,8192]{1,0:T(1,128)S(1)}, f32[1,8192]{1,0:T(1,128)S(1)}) custom-call(bf16[4096,256]{1,0:T(8,128)(2,1)S(1)} %copy-done.2, bf16[8192,256]{1,0:T(8,128)(2,1)} %all-gather.3.cloned.1.call-done.y_ref.src_ref), custom_call_target="tpu_custom_call" | custom-call | flops 17179869184 | bytes 6291456 | tf_op jit(solution)/shard_map/trans_stats/pallas_call | solution.py:92
  122.4 33.4 %all-gather = f32[16,1,8192]{2,1,0:T(1,128)S(1)} all-gather(f32[2,1,8192]{2,1,0:T(1,128)S(1)} %pad_maximum_fusion.1), channel_id=2, replica_groups=mesh['row'=4,'col'=8] {'col'}, dimensions={0}, use_global_device_ids=true | all-gather | bytes 589824 | tf_op jit(solution)/shard_map/all_gather | solution.py:352
  156.5 2.7 copy.15.top_ref
  159.3 2.2 copy-done.5
  161.5 14.2 %build_trans.4 = (bf16[8192,1280]{1,0:T(8,128)(2,1)}, f32[64,1280]{1,0:T(8,128)S(1)}) custom-call(bf16[8192,256]{1,0:T(8,128)(2,1)S(1)} %copy-done.5, bf16[1280,256]{1,0:T(8,128)(2,1)S(1)} %get-tuple-element.105.dst_ref, f32[8192,1]{1,0:T(8,128)} %copy.15.top_ref, bf16[64,8192]{1,0:T(8,128)(2,1)S(1)} %divide_convert_fusion.1.weight_ref), custom_call_target="tpu_custom_call" | custom-call | flops 6710886400 | bytes 20971520 | tf_op jit(solution)/shard_map/build_trans/pallas_call | solution.py:146
  176.4 14.3 %build_trans.5 = (bf16[8192,1280]{1,0:T(8,128)(2,1)}, f32[64,1280]{1,0:T(8,128)S(1)}) custom-call(bf16[8192,256]{1,0:T(8,128)(2,1)S(1)} %copy-done.5, bf16[1280,256]{1,0:T(8,128)(2,1)S(1)} %get-tuple-element.104.dst_ref, f32[8192,1]{1,0:T(8,128)} %copy.15.top_ref, bf16[64,8192]{1,0:T(8,128)(2,1)S(1)} %divide_convert_fusion.1.weight_ref), custom_call_target="tpu_custom_call" | custom-call | flops 6710886400 | bytes 20971520 | tf_op jit(solution)/shard_map/build_trans/pallas_call | solution.py:146
  192.3 12.8 %build_trans.6 = (bf16[8192,1024]{1,0:T(8,128)(2,1)}, f32[64,1024]{1,0:T(8,128)S(1)}) custom-call(bf16[8192,256]{1,0:T(8,128)(2,1)S(1)} %copy-done.5, bf16[1024,256]{1,0:T(8,128)(2,1)S(1)} %copy-done.3, f32[8192,1]{1,0:T(8,128)} %copy.15.top_ref, bf16[64,8192]{1,0:T(8,128)(2,1)S(1)} %divide_convert_fusion.1.weight_ref), custom_call_target="tpu_custom_call" | custom-call | flops 5368709120 | bytes 16777216 | tf_op jit(solution)/shard_map/build_trans/pallas_call | solution.py:146
  208.0 9.5 %build_trans.7 = (bf16[8192,512]{1,0:T(8,128)(2,1)}, f32[64,512]{1,0:T(8,128)S(1)}) custom-call(bf16[8192,256]{1,0:T(8,128)(2,1)S(1)} %copy-done.5, bf16[512,256]{1,0:T(8,128)(2,1)S(1)} %copy-done.4, f32[8192,1]{1,0:T(8,128)} %copy.15.top_ref, bf16[64,8192]{1,0:T(8,128)(2,1)S(1)} %divide_convert_fusion.1.weight_ref), custom_call_target="tpu_custom_call" | custom-call | flops 2684354560 | bytes 8388608 | tf_op jit(solution)/shard_map/build_trans/pallas_call | solution.py:146
  217.5 20.7 %collective-permute-done.3 = f32[64,1280]{1,0:T(8,128)S(1)} collective-permute-done((f32[64,1280]{1,0:T(8,128)S(1)}, f32[64,1280]{1,0:T(8,128)S(1)}, u32[]{:S(2)}, u32[]{:S(2)}) %collective-permute-start.3) | collective-permute-done | bytes 327712 | tf_op jit(solution)/shard_map/ppermute | solution.py:258
  242.3 6.1 %collective-permute-start.12 = (f32[64]{0:T(128)S(1)}, f32[64]{0:T(128)S(1)}, u32[]{:S(2)}, u32[]{:S(2)}) collective-permute-start(f32[64]{0:T(128)S(1)} %add.137), channel_id=1, source_target_pairs={{0,2},{1,3},{2,0},{3,1},{4,6},{5,7},{6,4},{7,5},{8,10},{9,11},{10,... | collective-permute-start | bytes 776 | tf_op jit(solution)/shard_map/ppermute | solution.py:211
  248.5 1.5 collective-permute-done.12
  250.0 6.6 %collective-permute-start.13 = (f32[64]{0:T(128)S(1)}, f32[64]{0:T(128)S(1)}, u32[]{:S(2)}, u32[]{:S(2)}) collective-permute-start(f32[64]{0:T(128)S(1)} %add.138), channel_id=1, source_target_pairs={{0,4},{1,5},{2,6},{3,7},{4,0},{5,1},{6,2},{7,3},{8,12},{9,13},{10,... | collective-permute-start | bytes 776 | tf_op jit(solution)/shard_map/ppermute | solution.py:211
  256.5 1.5 collective-permute-done.13
  259.5 2.7 collective-permute-start.17
  262.2 2.4 collective-permute-start.19
  265.4 1.5 collective-permute-done.17
  268.9 7.9 %collective-permute-done.22 = f32[64,512]{1,0:T(8,128)S(1)} collective-permute-done((f32[64,512]{1,0:T(8,128)S(1)}, f32[64,512]{1,0:T(8,128)S(1)}, u32[]{:S(2)}, u32[]{:S(2)}) %collective-permute-start.22) | collective-permute-done | bytes 131104 | tf_op jit(solution)/shard_map/ppermute | solution.py:258
  278.4 3.8 collective-permute-done.23
  282.3 2.0 collective-permute-start.25
  285.6 1.9 collective-permute-done.25
  287.5 2.9 collective-permute-start.26
  290.5 3.8 collective-permute-done.26
  296.1 2.0 collective-permute-done.27
  298.1 1.7 divide_convert_fusion.weight_ref
  299.8 8.9 %advance.4 = f32[64,1280]{1,0:T(8,128)S(1)} custom-call(bf16[64,8192]{1,0:T(8,128)(2,1)S(1)} %divide_convert_fusion.weight_ref, bf16[8192,1280]{1,0:T(8,128)(2,1)} %get-tuple-element.79.trans_ref), custom_call_target="tpu_custom_call" | custom-call | flops 1342177280 | bytes 20971520 | tf_op jit(solution)/shard_map/advance/pallas_call | solution.py:186
  308.7 4.6 %collective-permute-start.28 = (f32[64,1280]{1,0:T(8,128)S(1)}, f32[64,1280]{1,0:T(8,128)S(1)}, u32[]{:S(2)}, u32[]{:S(2)}) collective-permute-start(f32[64,1280]{1,0:T(8,128)S(1)} %advance.4), channel_id=1, source_target_pairs={{0,8},{24,16},{1,9},{25,17},{2,10},{26,18},{3,11},{27,19},{4,12},{... | collective-permute-start | bytes 983048 | tf_op jit(solution)/shard_map/ppermute | solution.py:264
  313.3 8.9 %advance.5 = f32[64,1280]{1,0:T(8,128)S(1)} custom-call(bf16[64,8192]{1,0:T(8,128)(2,1)S(1)} %divide_convert_fusion.weight_ref, bf16[8192,1280]{1,0:T(8,128)(2,1)} %get-tuple-element.80.trans_ref), custom_call_target="tpu_custom_call" | custom-call | flops 1342177280 | bytes 20971520 | tf_op jit(solution)/shard_map/advance/pallas_call | solution.py:186
  323.0 3.9 collective-permute-start.30
  326.9 7.7 %advance.6 = f32[64,1024]{1,0:T(8,128)S(1)} custom-call(bf16[64,8192]{1,0:T(8,128)(2,1)S(1)} %divide_convert_fusion.weight_ref, bf16[8192,1024]{1,0:T(8,128)(2,1)} %get-tuple-element.83.trans_ref), custom_call_target="tpu_custom_call" | custom-call | flops 1073741824 | bytes 16777216 | tf_op jit(solution)/shard_map/advance/pallas_call | solution.py:186
  335.4 1.4 collective-permute-start.32
  338.8 6.8 %collective-permute-start.33 = (f32[64,1024]{1,0:T(8,128)S(1)}, f32[64,1024]{1,0:T(8,128)}, u32[]{:S(2)}, u32[]{:S(2)}) collective-permute-start(f32[64,1024]{1,0:T(8,128)S(1)} %advance.6), channel_id=1, source_target_pairs={{0,8},{24,16},{1,9},{25,17},{2,10},{26,18},{3,11},{27,19},{4,12},{... | collective-permute-start | bytes 786440 | tf_op jit(solution)/shard_map/ppermute | solution.py:264
  345.5 5.0 %advance.7 = f32[64,512]{1,0:T(8,128)S(1)} custom-call(bf16[64,8192]{1,0:T(8,128)(2,1)S(1)} %divide_convert_fusion.weight_ref, bf16[8192,512]{1,0:T(8,128)(2,1)} %get-tuple-element.88.trans_ref), custom_call_target="tpu_custom_call" | custom-call | flops 536870912 | bytes 8388608 | tf_op jit(solution)/shard_map/advance/pallas_call | solution.py:186
  354.6 5.4 %collective-permute-start.36 = (f32[64,512]{1,0:T(8,128)S(1)}, f32[64,512]{1,0:T(8,128)S(1)}, u32[]{:S(2)}, u32[]{:S(2)}) collective-permute-start(f32[64,512]{1,0:T(8,128)S(1)} %advance.7), channel_id=1, source_target_pairs={{0,8},{24,16},{1,9},{25,17},{2,10},{26,18},{3,11},{27,19},{4,12},{... | collective-permute-start | bytes 393224 | tf_op jit(solution)/shard_map/ppermute | solution.py:264
  361.1 1.5 collective-permute-done.36
  365.3 6.2 %collective-permute-done.37 = f32[64,1024]{1,0:T(8,128)S(1)} collective-permute-done((f32[64,1024]{1,0:T(8,128)S(1)}, f32[64,1024]{1,0:T(8,128)S(1)}, u32[]{:S(2)}, u32[]{:S(2)}) %collective-permute-start.37) | collective-permute-done | bytes 262176 | tf_op jit(solution)/shard_map/ppermute | solution.py:267
  372.9 5.5 %collective-permute-done.39 = f32[64,512]{1,0:T(8,128)S(1)} collective-permute-done((f32[64,512]{1,0:T(8,128)S(1)}, f32[64,512]{1,0:T(8,128)S(1)}, u32[]{:S(2)}, u32[]{:S(2)}) %collective-permute-start.39) | collective-permute-done | bytes 131104 | tf_op jit(solution)/shard_map/ppermute | solution.py:267
  381.1 2.3 collective-permute-done.41
  383.4 2.0 collective-permute-start.42
  385.4 1.6 collective-permute-done.42
  (133 shorter events, 41.2 us)
Async XLA Ops:
  7.2 76.0 %all-gather.3.cloned.1.call-start = ((), (), s32[]{:S(2)}) async-start(), calls=%async_computation | async-start | bytes 4718592 | tf_op jit(solution)/shard_map/all_gather | solution.py:337
  11.7 56.6 %copy-start.9 = (s32[64,2]{0,1:T(2,128)S(1)}, s32[64,2]{0,1:T(2,128)}, u32[]{:S(2)}) copy-start(s32[64,2]{0,1:T(2,128)} %param.11) | copy-start | bytes 1540
  62.5 15.6 %collective-permute-start.10 = (f32[2,1,4096]{2,1,0:T(1,128)S(1)}, f32[2,1,4096]{2,1,0:T(1,128)S(1)}, u32[]{:S(2)}, u32[]{:S(2)}) collective-permute-start(f32[2,1,4096]{2,1,0:T(1,128)S(1)} %pad_maximum_fusion.2), channel_id=1, source_target_pairs={{0,24},{8,16},{16,8},{24,0},{1,25},{9,17},{17,9},{25,1},{2,26},{10... | collective-permute-start | bytes 98312 | tf_op jit(solution)/shard_map/ppermute | solution.py:211
  67.6 10.5 %collective-permute-start.8 = (f32[2,1,4096]{2,1,0:T(1,128)S(1)}, f32[2,1,4096]{2,1,0:T(1,128)S(1)}, u32[]{:S(2)}, u32[]{:S(2)}) collective-permute-start(f32[2,1,4096]{2,1,0:T(1,128)S(1)} %pad_maximum_fusion.2), channel_id=1, source_target_pairs={{0,8},{8,0},{16,24},{24,16},{1,9},{9,1},{17,25},{25,17},{2,10},{10... | collective-permute-start | bytes 98312 | tf_op jit(solution)/shard_map/ppermute | solution.py:211
  67.6 10.5 %collective-permute-start.9 = (f32[2,1,4096]{2,1,0:T(1,128)S(1)}, f32[2,1,4096]{2,1,0:T(1,128)}, u32[]{:S(2)}, u32[]{:S(2)}) collective-permute-start(f32[2,1,4096]{2,1,0:T(1,128)S(1)} %pad_maximum_fusion.2), channel_id=1, source_target_pairs={{0,16},{8,24},{16,0},{24,8},{1,17},{9,25},{17,1},{25,9},{2,18},{10... | collective-permute-start | bytes 98312 | tf_op jit(solution)/shard_map/ppermute | solution.py:211
  68.3 4.5 %copy-start.2 = (bf16[4096,256]{1,0:T(8,128)(2,1)S(1)}, bf16[4096,256]{1,0:T(8,128)(2,1)}, u32[]{:S(2)}) copy-start(bf16[4096,256]{1,0:T(8,128)(2,1)} %x_ref.2) | copy-start | bytes 6291460
  71.4 9.6 %copy-start.1 = (bf16[4096,256]{1,0:T(8,128)(2,1)S(1)}, bf16[4096,256]{1,0:T(8,128)(2,1)}, u32[]{:S(2)}) copy-start(bf16[4096,256]{1,0:T(8,128)(2,1)} %y_ref.1) | copy-start | bytes 6291460
  71.4 4.3 %collective-permute-start.6 = (bf16[128,256]{1,0:T(8,128)(2,1)S(1)}, bf16[128,256]{1,0:T(8,128)(2,1)S(1)}, u32[]{:S(2)}, u32[]{:S(2)}) collective-permute-start(bf16[128,256]{1,0:T(8,128)(2,1)S(1)} %fusion.3), channel_id=1, source_target_pairs={{0,8},{8,0},{16,24},{24,16},{1,9},{9,1},{17,25},{25,17},{2,10},{10... | collective-permute-start | bytes 196616 | tf_op jit(solution)/shard_map/ppermute | solution.py:211
  75.8 5.2 %collective-permute-start.7 = (bf16[128,256]{1,0:T(8,128)(2,1)S(1)}, bf16[128,256]{1,0:T(8,128)(2,1)S(1)}, u32[]{:S(2)}, u32[]{:S(2)}) collective-permute-start(bf16[128,256]{1,0:T(8,128)(2,1)S(1)} %add.128), channel_id=1, source_target_pairs={{0,16},{8,24},{16,0},{24,8},{1,17},{9,25},{17,1},{25,9},{2,18},{10... | collective-permute-start | bytes 196616 | tf_op jit(solution)/shard_map/ppermute | solution.py:211
  175.7 15.1 %collective-permute-start = (f32[64,1280]{1,0:T(8,128)S(1)}, f32[64,1280]{1,0:T(8,128)S(1)}, u32[]{:S(2)}, u32[]{:S(2)}) collective-permute-start(f32[64,1280]{1,0:T(8,128)S(1)} %get-tuple-element.53), channel_id=1, source_target_pairs={{24,16},{25,17},{2,10},{26,18},{3,11},{27,19},{4,12},{28,20},{5,13... | collective-permute-start | bytes 983048 | tf_op jit(solution)/shard_map/ppermute | solution.py:258
  176.4 14.3 %copy-start.7 = (f32[128,4096]{1,0:T(8,128)S(1)}, f32[128,4096]{1,0:T(8,128)}, u32[]{:S(2)}) copy-start(f32[128,4096]{1,0:T(8,128)} %fusion) | copy-start | bytes 6291460
  190.9 14.2 %collective-permute-start.1 = (f32[64,1280]{1,0:T(8,128)S(1)}, f32[64,1280]{1,0:T(8,128)S(1)}, u32[]{:S(2)}, u32[]{:S(2)}) collective-permute-start(f32[64,1280]{1,0:T(8,128)S(1)} %add.123), channel_id=1, source_target_pairs={{16,8},{17,9},{18,10},{19,11},{12,20},{13,21},{14,22},{15,23}} | collective-permute-start | bytes 983048 | tf_op jit(solution)/shard_map/ppermute | solution.py:258
  191.6 13.5 %collective-permute-start.2 = (f32[64,1280]{1,0:T(8,128)S(1)}, f32[64,1280]{1,0:T(8,128)S(1)}, u32[]{:S(2)}, u32[]{:S(2)}) collective-permute-start(f32[64,1280]{1,0:T(8,128)S(1)} %get-tuple-element.58), channel_id=1, source_target_pairs={{24,16},{25,17},{2,10},{26,18},{3,11},{27,19},{4,12},{28,20},{5,13... | collective-permute-start | bytes 983048 | tf_op jit(solution)/shard_map/ppermute | solution.py:258
  205.2 12.3 %collective-permute-start.4 = (f32[64,1280]{1,0:T(8,128)S(1)}, f32[64,1280]{1,0:T(8,128)S(1)}, u32[]{:S(2)}, u32[]{:S(2)}) collective-permute-start(f32[64,1280]{1,0:T(8,128)S(1)} %add.125), channel_id=1, source_target_pairs={{16,8},{17,9},{18,10},{19,11},{12,20},{13,21},{14,22},{15,23}} | collective-permute-start | bytes 983048 | tf_op jit(solution)/shard_map/ppermute | solution.py:258
  205.9 32.4 %collective-permute-start.3 = (f32[64,1280]{1,0:T(8,128)S(1)}, f32[64,1280]{1,0:T(8,128)S(1)}, u32[]{:S(2)}, u32[]{:S(2)}) collective-permute-start(f32[64,1280]{1,0:T(8,128)S(1)} %add.124), channel_id=1, source_target_pairs={{8,0},{9,1},{22,30},{23,31}} | collective-permute-start | bytes 983048 | tf_op jit(solution)/shard_map/ppermute | solution.py:258
  207.2 10.3 %collective-permute-start.5 = (f32[64,1024]{1,0:T(8,128)S(1)}, f32[64,1024]{1,0:T(8,128)S(1)}, u32[]{:S(2)}, u32[]{:S(2)}) collective-permute-start(f32[64,1024]{1,0:T(8,128)S(1)} %get-tuple-element.63), channel_id=1, source_target_pairs={{24,16},{25,17},{2,10},{26,18},{3,11},{27,19},{4,12},{28,20},{5,13... | collective-permute-start | bytes 786440 | tf_op jit(solution)/shard_map/ppermute | solution.py:258
  238.3 19.8 %collective-permute-start.15 = (f32[64,1024]{1,0:T(8,128)S(1)}, f32[64,1024]{1,0:T(8,128)S(1)}, u32[]{:S(2)}, u32[]{:S(2)}) collective-permute-start(f32[64,1024]{1,0:T(8,128)S(1)} %add.140), channel_id=1, source_target_pairs={{16,8},{17,9},{18,10},{19,11},{12,20},{13,21},{14,22},{15,23}} | collective-permute-start | bytes 786440 | tf_op jit(solution)/shard_map/ppermute | solution.py:258
  239.0 19.1 %collective-permute-start.14 = (f32[64,1280]{1,0:T(8,128)S(1)}, f32[64,1280]{1,0:T(8,128)S(1)}, u32[]{:S(2)}, u32[]{:S(2)}) collective-permute-start(f32[64,1280]{1,0:T(8,128)S(1)} %add.127), channel_id=1, source_target_pairs={{8,0},{9,1},{22,30},{23,31}} | collective-permute-start | bytes 983048 | tf_op jit(solution)/shard_map/ppermute | solution.py:258
  240.4 17.7 %collective-permute-start.16 = (f32[64,512]{1,0:T(8,128)S(1)}, f32[64,512]{1,0:T(8,128)S(1)}, u32[]{:S(2)}, u32[]{:S(2)}) collective-permute-start(f32[64,512]{1,0:T(8,128)S(1)} %get-tuple-element.69), channel_id=1, source_target_pairs={{24,16},{25,17},{2,10},{26,18},{3,11},{27,19},{4,12},{28,20},{5,13... | collective-permute-start | bytes 393224 | tf_op jit(solution)/shard_map/ppermute | solution.py:258
  241.1 1.2 collective-permute-start.11
  242.3 7.7 %collective-permute-start.12 = (f32[64]{0:T(128)S(1)}, f32[64]{0:T(128)S(1)}, u32[]{:S(2)}, u32[]{:S(2)}) collective-permute-start(f32[64]{0:T(128)S(1)} %add.137), channel_id=1, source_target_pairs={{0,2},{1,3},{2,0},{3,1},{4,6},{5,7},{6,4},{7,5},{8,10},{9,11},{10,... | collective-permute-start | bytes 776 | tf_op jit(solution)/shard_map/ppermute | solution.py:211
  250.0 8.1 %collective-permute-start.13 = (f32[64]{0:T(128)S(1)}, f32[64]{0:T(128)S(1)}, u32[]{:S(2)}, u32[]{:S(2)}) collective-permute-start(f32[64]{0:T(128)S(1)} %add.138), channel_id=1, source_target_pairs={{0,4},{1,5},{2,6},{3,7},{4,0},{5,1},{6,2},{7,3},{8,12},{9,13},{10,... | collective-permute-start | bytes 776 | tf_op jit(solution)/shard_map/ppermute | solution.py:211
  258.2 9.4 %collective-permute-start.20 = (f32[64,1024]{1,0:T(8,128)S(1)}, f32[64,1024]{1,0:T(8,128)S(1)}, u32[]{:S(2)}, u32[]{:S(2)}) collective-permute-start(f32[64,1024]{1,0:T(8,128)S(1)} %add.142), channel_id=1, source_target_pairs={{8,0},{9,1},{22,30},{23,31}} | collective-permute-start | bytes 786440 | tf_op jit(solution)/shard_map/ppermute | solution.py:258
  259.5 7.4 %collective-permute-start.17 = (f32[64]{0:T(128)S(1)}, f32[64]{0:T(128)S(1)}, u32[]{:S(2)}, u32[]{:S(2)}) collective-permute-start(f32[64]{0:T(128)S(1)} %add.139), channel_id=1, source_target_pairs={{0,8},{8,0},{16,24},{24,16},{1,9},{9,1},{17,25},{25,17},{2,10},{10... | collective-permute-start | bytes 776 | tf_op jit(solution)/shard_map/ppermute | solution.py:211
  262.2 4.6 %collective-permute-start.18 = (f32[64]{0:T(128)S(1)}, f32[64]{0:T(128)S(1)}, u32[]{:S(2)}, u32[]{:S(2)}) collective-permute-start(f32[64]{0:T(128)S(1)} %add.139), channel_id=1, source_target_pairs={{0,16},{8,24},{16,0},{24,8},{1,17},{9,25},{17,1},{25,9},{2,18},{10... | collective-permute-start | bytes 776 | tf_op jit(solution)/shard_map/ppermute | solution.py:211
  262.2 5.3 %collective-permute-start.19 = (f32[64]{0:T(128)S(1)}, f32[64]{0:T(128)S(1)}, u32[]{:S(2)}, u32[]{:S(2)}) collective-permute-start(f32[64]{0:T(128)S(1)} %add.139), channel_id=1, source_target_pairs={{0,24},{8,16},{16,8},{24,0},{1,25},{9,17},{17,9},{25,1},{2,26},{10... | collective-permute-start | bytes 776 | tf_op jit(solution)/shard_map/ppermute | solution.py:211
  264.7 2.9 collective-permute-start.21
  267.6 9.2 %collective-permute-start.22 = (f32[64,512]{1,0:T(8,128)S(1)}, f32[64,512]{1,0:T(8,128)S(1)}, u32[]{:S(2)}, u32[]{:S(2)}) collective-permute-start(f32[64,512]{1,0:T(8,128)S(1)} %add.148), channel_id=1, source_target_pairs={{8,0},{9,1},{22,30},{23,31}} | collective-permute-start | bytes 393224 | tf_op jit(solution)/shard_map/ppermute | solution.py:258
  277.1 5.2 %collective-permute-start.23 = (bf16[64,2048]{1,0:T(8,128)(2,1)S(1)}, bf16[64,2048]{1,0:T(8,128)(2,1)S(1)}, u32[]{:S(2)}, u32[]{:S(2)}) collective-permute-start(bf16[64,2048]{1,0:T(8,128)(2,1)S(1)} %slice.97), channel_id=1, source_target_pairs={{0,2},{1,3},{10,8},{11,9},{20,22},{21,23},{30,28},{31,29}} | collective-permute-start | bytes 786440 | tf_op jit(solution)/shard_map/ppermute | solution.py:311
  282.3 5.2 %collective-permute-start.25 = (bf16[64,2048]{1,0:T(8,128)(2,1)S(1)}, bf16[64,2048]{1,0:T(8,128)(2,1)}, u32[]{:S(2)}, u32[]{:S(2)}) collective-permute-start(bf16[64,2048]{1,0:T(8,128)(2,1)S(1)} %get-tuple-element.107), channel_id=1, source_target_pairs={{0,4},{1,5},{10,14},{11,15},{20,16},{21,17},{30,26},{31,27}} | collective-permute-start | bytes 786440 | tf_op jit(solution)/shard_map/ppermute | solution.py:311
  284.3 6.1 %collective-permute-start.24 = (bf16[64,2048]{1,0:T(8,128)(2,1)S(1)}, bf16[64,2048]{1,0:T(8,128)(2,1)S(1)}, u32[]{:S(2)}, u32[]{:S(2)}) collective-permute-start(bf16[64,2048]{1,0:T(8,128)(2,1)S(1)} %get-tuple-element.106), channel_id=1, source_target_pairs={{0,4},{1,5},{2,6},{3,7},{10,14},{11,15},{8,12},{9,13},{20,16},{21,... | collective-permute-start | bytes 786440 | tf_op jit(solution)/shard_map/ppermute | solution.py:311
  287.5 6.7 %collective-permute-start.26 = (bf16[64,2048]{1,0:T(8,128)(2,1)S(1)}, bf16[64,2048]{1,0:T(8,128)(2,1)S(1)}, u32[]{:S(2)}, u32[]{:S(2)}) collective-permute-start(bf16[64,2048]{1,0:T(8,128)(2,1)S(1)} %broadcast_select_fusion.1), channel_id=1, source_target_pairs={{0,2},{1,3},{4,6},{5,7},{10,8},{11,9},{14,12},{15,13},{20,22},{21,... | collective-permute-start | bytes 786440 | tf_op jit(solution)/shard_map/ppermute | solution.py:311
  296.0 2.1 collective-permute-start.27
  308.7 13.5 %collective-permute-start.28 = (f32[64,1280]{1,0:T(8,128)S(1)}, f32[64,1280]{1,0:T(8,128)S(1)}, u32[]{:S(2)}, u32[]{:S(2)}) collective-permute-start(f32[64,1280]{1,0:T(8,128)S(1)} %advance.4), channel_id=1, source_target_pairs={{0,8},{24,16},{1,9},{25,17},{2,10},{26,18},{3,11},{27,19},{4,12},{... | collective-permute-start | bytes 983048 | tf_op jit(solution)/shard_map/ppermute | solution.py:264
  322.3 12.3 %collective-permute-start.29 = (f32[64,1280]{1,0:T(8,128)S(1)}, f32[64,1280]{1,0:T(8,128)S(1)}, u32[]{:S(2)}, u32[]{:S(2)}) collective-permute-start(f32[64,1280]{1,0:T(8,128)S(1)} %add.150), channel_id=1, source_target_pairs={{8,16},{16,8},{9,17},{17,9},{10,18},{18,10},{11,19},{19,11},{12,20... | collective-permute-start | bytes 983048 | tf_op jit(solution)/shard_map/ppermute | solution.py:265
  323.0 11.6 %collective-permute-start.30 = (f32[64,1280]{1,0:T(8,128)S(1)}, f32[64,1280]{1,0:T(8,128)S(1)}, u32[]{:S(2)}, u32[]{:S(2)}) collective-permute-start(f32[64,1280]{1,0:T(8,128)S(1)} %advance.5), channel_id=1, source_target_pairs={{0,8},{24,16},{1,9},{25,17},{2,10},{26,18},{3,11},{27,19},{4,12},{... | collective-permute-start | bytes 983048 | tf_op jit(solution)/shard_map/ppermute | solution.py:264
  335.4 15.2 %collective-permute-start.32 = (f32[64,1280]{1,0:T(8,128)}, f32[64,1280]{1,0:T(8,128)}, u32[]{:S(2)}, u32[]{:S(2)}) collective-permute-start(f32[64,1280]{1,0:T(8,128)} %add.152), channel_id=1, source_target_pairs={{8,16},{16,8},{9,17},{17,9},{10,18},{18,10},{11,19},{19,11},{12,20... | collective-permute-start | bytes 983048 | tf_op jit(solution)/shard_map/ppermute | solution.py:265
  337.5 13.1 %collective-permute-start.31 = (f32[64,1280]{1,0:T(8,128)}, f32[64,1280]{1,0:T(8,128)}, u32[]{:S(2)}, u32[]{:S(2)}) collective-permute-start(f32[64,1280]{1,0:T(8,128)} %add.151), channel_id=1, source_target_pairs={{8,0},{16,24},{9,1},{17,25},{10,2},{18,26},{11,3},{19,27},{12,4},{... | collective-permute-start | bytes 983048 | tf_op jit(solution)/shard_map/ppermute | solution.py:267
  338.8 11.8 %collective-permute-start.33 = (f32[64,1024]{1,0:T(8,128)S(1)}, f32[64,1024]{1,0:T(8,128)}, u32[]{:S(2)}, u32[]{:S(2)}) collective-permute-start(f32[64,1024]{1,0:T(8,128)S(1)} %advance.6), channel_id=1, source_target_pairs={{0,8},{24,16},{1,9},{25,17},{2,10},{26,18},{3,11},{27,19},{4,12},{... | collective-permute-start | bytes 786440 | tf_op jit(solution)/shard_map/ppermute | solution.py:264
  351.6 11.0 %collective-permute-start.35 = (f32[64,1024]{1,0:T(8,128)S(1)}, f32[64,1024]{1,0:T(8,128)S(1)}, u32[]{:S(2)}, u32[]{:S(2)}) collective-permute-start(f32[64,1024]{1,0:T(8,128)S(1)} %add.154), channel_id=1, source_target_pairs={{8,16},{16,8},{9,17},{17,9},{10,18},{18,10},{11,19},{19,11},{12,20... | collective-permute-start | bytes 786440 | tf_op jit(solution)/shard_map/ppermute | solution.py:265
  353.3 9.9 %collective-permute-start.34 = (f32[64,1280]{1,0:T(8,128)S(1)}, f32[64,1280]{1,0:T(8,128)S(1)}, u32[]{:S(2)}, u32[]{:S(2)}) collective-permute-start(f32[64,1280]{1,0:T(8,128)S(1)} %add.153), channel_id=1, source_target_pairs={{8,0},{16,24},{9,1},{17,25},{10,2},{18,26},{11,3},{19,27},{12,4},{... | collective-permute-start | bytes 983048 | tf_op jit(solution)/shard_map/ppermute | solution.py:267
  354.6 7.9 %collective-permute-start.36 = (f32[64,512]{1,0:T(8,128)S(1)}, f32[64,512]{1,0:T(8,128)S(1)}, u32[]{:S(2)}, u32[]{:S(2)}) collective-permute-start(f32[64,512]{1,0:T(8,128)S(1)} %advance.7), channel_id=1, source_target_pairs={{0,8},{24,16},{1,9},{25,17},{2,10},{26,18},{3,11},{27,19},{4,12},{... | collective-permute-start | bytes 393224 | tf_op jit(solution)/shard_map/ppermute | solution.py:264
  363.3 8.3 %collective-permute-start.37 = (f32[64,1024]{1,0:T(8,128)S(1)}, f32[64,1024]{1,0:T(8,128)S(1)}, u32[]{:S(2)}, u32[]{:S(2)}) collective-permute-start(f32[64,1024]{1,0:T(8,128)S(1)} %add.155), channel_id=1, source_target_pairs={{8,0},{16,24},{9,1},{17,25},{10,2},{18,26},{11,3},{19,27},{12,4},{... | collective-permute-start | bytes 786440 | tf_op jit(solution)/shard_map/ppermute | solution.py:267
  364.6 0.7 collective-permute-start.38
  371.6 6.9 %collective-permute-start.39 = (f32[64,512]{1,0:T(8,128)S(1)}, f32[64,512]{1,0:T(8,128)S(1)}, u32[]{:S(2)}, u32[]{:S(2)}) collective-permute-start(f32[64,512]{1,0:T(8,128)S(1)} %add.157), channel_id=1, source_target_pairs={{8,0},{16,24},{9,1},{17,25},{10,2},{18,26},{11,3},{19,27},{12,4},{... | collective-permute-start | bytes 393224 | tf_op jit(solution)/shard_map/ppermute | solution.py:267
  378.7 1.2 collective-permute-start.40
  379.9 3.5 collective-permute-start.41
  383.4 3.5 collective-permute-start.42
  (6 other events, 13.1 us)
Sparse Core Ops, SparseCore 0:
  9.9 39.5 all-gather.2

commit v2 on v1

--- a/solution.py
+++ b/solution.py
@@ -171,25 +171,30 @@
     )(src, dst, top, weights)
 
 
-def advance_kernel(weight_ref, trans_ref, out_ref):
+def advance_kernel(weight_ref, *refs):
+    trans_refs, out_ref = refs[:-1], refs[-1]
+
     @pl.when(pl.program_id(0) == 0)
     def _():
         out_ref[...] = jnp.zeros_like(out_ref)
 
-    out_ref[...] += jnp.dot(weight_ref[...], trans_ref[...], preferred_element_type=F32)
+    at = 0
+    for trans_ref in trans_refs:
+        here = slice(at, at + trans_ref.shape[1])
+        out_ref[:, here] += jnp.dot(weight_ref[...], trans_ref[...], preferred_element_type=F32)
+        at += trans_ref.shape[1]
 
 
 def advance(weights, trans):
-    sources, dests = trans.shape
+    sources = trans[0].shape[0]
+    dests = sum(part.shape[1] for part in trans)
     batch = weights.shape[0]
-    rows = block_of(sources, 2048)
+    rows = block_of(sources, 1024)
     return pl.pallas_call(
         advance_kernel,
         grid=(sources // rows,),
-        in_specs=[
-            pl.BlockSpec((batch, rows), lambda i: (0, i)),
-            pl.BlockSpec((rows, dests), lambda i: (i, 0)),
-        ],
+        in_specs=[pl.BlockSpec((batch, rows), lambda i: (0, i))]
+        + [pl.BlockSpec((rows, part.shape[1]), lambda i: (i, 0)) for part in trans],
         out_specs=pl.BlockSpec((batch, dests), lambda i: (0, 0)),
         out_shape=jax.ShapeDtypeStruct((batch, dests), F32),
         compiler_params=params(),
@@ -199,7 +204,7 @@
             transcendentals=0,
         ),
         name="advance",
-    )(weights, trans)
+    )(weights, *trans)
 
 
 def bits_of(count):
@@ -234,64 +239,60 @@
 def widths_of(dests):
     unit = block_of(dests, 256)
     count = dests // unit
-    last = max(1, count // 8)
-    rest = count - last
-    first = [rest // 3 + (k < rest % 3) for k in range(3)]
-    return [unit * size for size in first + [last] if size]
-
-
-def add(value, received):
-    return value + received
+    first = max(1, count * 5 // 8)
+    return [unit * size for size in (first, count - first) if size]
 
 
 def root_hops(rows, cols):
     per_row = cols // rows
+    if rows == 4:
+        lines = {
+            0: ([(1, 0), (3, 2)], [(2, 0)]),
+            1: ([(0, 1), (3, 2)], [(2, 1)]),
+            2: ([(0, 1), (3, 2)], [(1, 2)]),
+            3: ([(0, 1), (2, 3)], [(1, 3)]),
+        }
+    else:
+        lines = {
+            root: [[(at, root)] for at in range(rows) if at != root] for root in range(rows)
+        }
     hops = []
-    for hop in range(1, rows):
-        perm = []
-        for col in range(cols):
-            root = col // per_row
-            if hop <= root:
-                perm.append(((hop - 1) * cols + col, hop * cols + col))
-            if hop <= rows - 1 - root:
-                perm.append(((rows - hop) * cols + col, (rows - hop - 1) * cols + col))
-        hops.append((lambda value, perm=perm: lax.ppermute(value, ("row", "col"), perm), add))
+    for hop in range(len(lines[0])):
+        perm = [
+            (a * cols + col, b * cols + col)
+            for col in range(cols)
+            for a, b in lines[col // per_row][hop]
+        ]
+        hops.append(lambda value, perm=perm: lax.ppermute(value, ("row", "col"), perm))
     return hops
-
-
-def everywhere_hops(middle):
-    return [
-        (lambda value: lax.ppermute(value, "row", [(0, 1), (3, 2)]), add),
-        (lambda value: lax.ppermute(value, "row", [(1, 2), (2, 1)]), add),
-        (
-            lambda value: lax.ppermute(value, "row", [(1, 0), (2, 3)]),
-            lambda value, received: jnp.where(middle, value, received),
-        ),
-    ]
 
 
 def piped(compute, operand, count, hops, small, rounds):
     moving, ready = [], []
+
+    def moved(beside):
+        received = [hops[at](value) for value, at in moving if at < len(hops)]
+        beside, *received = lax.optimization_barrier((beside(), *received))
+        received.reverse()
+        return beside, [
+            (value + received.pop(), at + 1) if at < len(hops) else (value, at)
+            for value, at in moving
+        ]
+
     for k in range(count):
-        part = compute(k, tied(operand, ready) if ready else operand)
-        received = [hops[at][0](value) if at < len(hops) else value for value, at in moving]
-        part, *received = lax.optimization_barrier((part, *received))
-        moving = [
-            (hops[at][1](value, got), at + 1) if at < len(hops) else (value, at)
-            for (value, at), got in zip(moving, received)
-        ]
+        part, moving = moved(lambda: compute(k, tied(operand, ready) if ready else operand))
         ready = [value for value, at in moving]
         moving.append((part, 0))
     small = small()
     for k in range(len(hops)):
-        received = [hops[at][0](value) if at < len(hops) else value for value, at in moving]
-        for step in rounds[k]:
-            small = step(small)
-        small, *received = lax.optimization_barrier((small, *received))
-        moving = [
-            (hops[at][1](value, got), at + 1) if at < len(hops) else (value, at)
-            for (value, at), got in zip(moving, received)
-        ]
+
+        def beside():
+            value = small
+            for step in rounds[k]:
+                value = step(value)
+            return value
+
+        small, moving = moved(beside)
     return [value for value, at in moving], small
 
 
@@ -310,10 +311,14 @@
         ]
         return lax.ppermute(value, ("row", "col"), perm)
 
-    first = jnp.where(relation == 0, first, sent(first, [(0, 1)]))
-    second = jnp.where(relation == 0, second, sent(second, [(0, 2)]))
-    first = jnp.where(relation <= 1, first, sent(first, [(0, 2), (1, 3)]))
-    second = jnp.where((relation == 0) | (relation == 2), second, sent(second, [(0, 1), (2, 3)]))
+    near, far = lax.optimization_barrier((sent(first, [(0, 1)]), sent(second, [(0, 2)])))
+    first = jnp.where(relation == 0, first, near)
+    second = jnp.where(relation == 0, second, far)
+    far, near = lax.optimization_barrier(
+        (sent(first, [(0, 2), (1, 3)]), sent(second, [(0, 1), (2, 3)]))
+    )
+    first = jnp.where(relation <= 1, first, far)
+    second = jnp.where((relation == 0) | (relation == 2), second, near)
     blocks = jnp.concatenate([first, second], axis=1)
     member = col % per_row
     for mask in bits_of(per_row):
@@ -329,7 +334,6 @@
 def on_device(src_emb, dst_emb, state_emb, word_emb, start_probs, token_ids):
     rows, cols = lax.axis_size("row"), lax.axis_size("col")
     row = lax.axis_index("row")
-    middle = (row == 1) | (row == 2)
     batch, steps = token_ids.shape
     dests = dst_emb.shape[0]
     states = dests * cols
@@ -361,15 +365,16 @@
 
     trans, scales1 = [], []
 
-    def add_over(axis, mask):
-        return lambda value: value + swapped(value, axis, mask)
-
     def add_rows(value):
         if rows != 4:
             return summed_all(value, ("row",))
         one, two, three = [swapped(value, "row", mask) for mask in (1, 2, 3)]
         return (value + one) + (two + three)
 
+
+    def add_over(axis, mask):
+        return lambda value: value + swapped(value, axis, mask)
+
     col_rounds = [add_over("col", mask) for mask in bits_of(cols)]
 
     def first_step(k, weights):
@@ -378,13 +383,14 @@
         scales1.append(jnp.sum(part * emit[:batch, here[k]], axis=1))
         return part
 
+    rounds = [col_rounds, [add_rows]] + [[]] * rows
     sums1, scale1 = piped(
         first_step,
         weights0,
         len(widths),
         root_hops(rows, cols),
         lambda: sum(scales1),
-        [col_rounds, [add_rows], []],
+        rounds,
     )
     scale1 = scale1 / states
     joint1 = jnp.concatenate(sums1, axis=1) * emit[:batch]
@@ -392,20 +398,11 @@
     source_probs = to_sources(probs1, rows, cols)
     weights1 = (source_probs.astype(F32) / row_total).astype(BF16)
 
-    def second_step(k, weights):
-        return advance(weights, trans[k])
-
-    sums2, _ = piped(
-        second_step,
-        weights1,
-        len(widths),
-        everywhere_hops(middle),
-        lambda: scale1,
-        [[], [], []],
-    )
-    joint2 = jnp.concatenate(sums2, axis=1) * emit[batch : 2 * batch]
-    scale2 = summed_all(jnp.sum(joint2, axis=1), ("col",)) / states
-    final_probs = joint2 / scale2[:, None]
+    part = advance(weights1, trans)
+    sums2 = lax.psum(part, "row")
+    scale2 = summed_all(jnp.sum(part * emit[batch : 2 * batch], axis=1), ("col", "row"))
+    scale2 = scale2 / states
+    final_probs = sums2 * emit[batch : 2 * batch] / scale2[:, None]
     log_norm = jnp.log(scale1) + jnp.log(scale2)
     return (final_probs, log_norm)
 

time: 393 us -> 379 us (0.964)
  blocking collectives: 33.4 us -> 8.73 us
  waiting for transfers between devices: 69.3 us -> 83.1 us
  Pallas kernels: 171 us -> 184 us
  starting transfers between devices: 78.2 us -> 70.6 us
  local copies, waits for them, and re-layouts: 10.4 us -> 6.01 us
  other arithmetic: 13 us -> 8.95 us
    psum x0 -> x1, waiting for transfers between devices: none -> 35.6 us  [on_device(): sums2 = lax.psum(part, 'row')]
    ppermute x12 -> x0, starting transfers between devices: 29.3 us -> none  [the longest x4 20.7 us: everywhere_hops(): lax.ppermute(value, 'row', [(0, 1), (3, 2)])]
    pallas_call x2, Pallas kernels: 89.9 us -> 117 us  [column_stats(): pl.pallas_call(functools.partial(stats_kernel, rows=rows, sub=sub), grid=...]
    all_gather x1, blocking collectives: 33.4 us -> 8.73 us  [on_device(): every = lax.all_gather(stats, 'col')]
    ppermute x15 -> x17, starting transfers between devices: 30.8 us -> 54.2 us  [swapped(): return lax.ppermute(value, axis, [(i, i ^ mask) for i in range(count)])]
    ppermute x12 -> x4, waiting for transfers between devices: 28.7 us -> 11.7 us  [root_hops(): lax.ppermute(value, ('row', 'col'), perm)]
    ppermute x12 -> x0, waiting for transfers between devices: 13.9 us -> none  [the longest x4 12.4 us: everywhere_hops(): lax.ppermute(value, 'row', [(1, 0), (2, 3)])]
    ppermute x15 -> x17, waiting for transfers between devices: 16.6 us -> 26.5 us  [swapped(): return lax.ppermute(value, axis, [(i, i ^ mask) for i in range(count)])]
  transfers between devices with their start and end apart: 44 -> 27, of which waited for: 20 -> 17; matrix products, arithmetic and copies ran while one was open for 3% -> 3% of each run, Pallas kernels for 28% -> 42%
where the time goes in v2:
time: 379 us; the launch traced here: 380 us
  Pallas kernels  184 us (49%)
  waiting for transfers between devices  83.1 us (22%)
  starting transfers between devices  70.6 us (19%)
  between operations  14.4 us (4%)
  other arithmetic  8.95 us (2%)
  blocking collectives  8.73 us (2%)
  local copies, waits for them, and re-layouts  6.01 us (2%)
  matrix products  4.73 us (1%)
    pallas_call x2, Pallas kernels, column_stats(): pl.pallas_call(functools.partial(stats_kernel, rows=rows, sub=sub), grid=...  117 us
    ppermute x17, starting transfers between devices, swapped(): return lax.ppermute(value, axis, [(i, i ^ mask) for i in range(count)])  54.2 us
    pallas_call x2, Pallas kernels, build_and_advance(): pl.pallas_call(functools.partial(trans_kernel, cols=cols), grid=(sources...  42.4 us
    psum x1, waiting for transfers between devices, on_device(): sums2 = lax.psum(part, 'row')  35.6 us
    ppermute x17, waiting for transfers between devices, swapped(): return lax.ppermute(value, axis, [(i, i ^ mask) for i in range(count)])  26.5 us
    pallas_call x1, Pallas kernels, advance(): pl.pallas_call(advance_kernel, grid=(sources // rows,), in_specs=[pl.Bloc...  24.1 us
    ppermute x4, waiting for transfers between devices, root_hops(): lax.ppermute(value, ('row', 'col'), perm)  11.7 us
    ppermute x4, starting transfers between devices, sent(): return lax.ppermute(value, ('row', 'col'), perm)  10.8 us
  transfers between devices with their start and end apart: 27, of which 17 were waited for; matrix products, arithmetic and copies ran while one was open for 3% of the time, Pallas kernels for 42%

profile of v2, /device:TPU:0, one launch (start us, length us, event | category | flops | bytes accessed | tf_op | source)
XLA Modules:
  0.0 380.2 jit_solution(5568778218356591574)
XLA Ops:
  8.7 3.1 fusion.3
  11.8 3.1 collective-permute-start.1
  14.8 2.2 copy-done.4
  17.0 78.1 %vocab_stats.1 = (f32[1,4096]{1,0:T(1,128)S(1)}, f32[1,4096]{1,0:T(1,128)S(1)}) custom-call(bf16[8000,256]{1,0:T(8,128)(2,1)S(1)} %copy-done.4, bf16[4096,256]{1,0:T(8,128)(2,1)S(1)} %copy-done.1), custom_call_target="tpu_custom_call" | custom-call | flops 16777216000 | bytes 6193152 | tf_op jit(solution)/shard_map/vocab_stats/pallas_call | solution.py:92
  95.2 30.0 %collective-permute-start.4 = (f32[2,1,4096]{2,1,0:T(1,128)S(1)}, f32[2,1,4096]{2,1,0:T(1,128)}, u32[]{:S(2)}, u32[]{:S(2)}) collective-permute-start(f32[2,1,4096]{2,1,0:T(1,128)S(1)} %pad_maximum_fusion.2), channel_id=1, source_target_pairs={{0,16},{8,24},{16,0},{24,8},{1,17},{9,25},{17,1},{25,9},{2,18},{10... | collective-permute-start | bytes 98312 | tf_op jit(solution)/shard_map/ppermute | solution.py:216
  125.2 1.4 collective-permute-start.5
  126.7 0.9 slice.56.dst_ref
  127.7 2.1 collective-permute-start.2
  129.8 39.2 %trans_stats.1 = (f32[1,8192]{1,0:T(1,128)S(1)}, f32[1,8192]{1,0:T(1,128)S(1)}) custom-call(bf16[4096,256]{1,0:T(8,128)(2,1)S(1)} %copy-done, bf16[8192,256]{1,0:T(8,128)(2,1)} %all-gather.3.cloned.1.call-done.y_ref.src_ref), custom_call_target="tpu_custom_call" | custom-call | flops 17179869184 | bytes 6291456 | tf_op jit(solution)/shard_map/trans_stats/pallas_call | solution.py:92
  169.0 8.7 %all-gather = f32[16,1,8192]{2,1,0:T(1,128)S(1)} all-gather(f32[2,1,8192]{2,1,0:T(1,128)S(1)} %pad_maximum_fusion.1), channel_id=2, replica_groups=mesh['row'=4,'col'=8] {'col'}, dimensions={0}, use_global_device_ids=true | all-gather | bytes 589824 | tf_op jit(solution)/shard_map/all_gather | solution.py:356
  178.4 2.7 copy.13.top_ref
  181.3 25.1 %build_trans.2 = (bf16[8192,2560]{1,0:T(8,128)(2,1)}, f32[64,2560]{1,0:T(8,128)S(1)}) custom-call(bf16[8192,256]{1,0:T(8,128)(2,1)} %all-gather.3.cloned.1.call-done.y_ref.src_ref, bf16[2560,256]{1,0:T(8,128)(2,1)S(1)} %slice.53.dst_ref, f32[8192,1]{1,0:T(8,128)} %copy.13.top_ref, bf16[64,8192]{1,0:T(8,128)(2,1)S(1)} %divide_convert_fusion.1.weight_ref), custom_call_target="tpu_custom_call" | custom-call | flops 13421772800 | bytes 41943040 | tf_op jit(solution)/shard_map/build_trans/pallas_call | solution.py:146
  206.4 1.3 collective-permute-start
  207.7 17.4 %build_trans.3 = (bf16[8192,1536]{1,0:T(8,128)(2,1)}, f32[64,1536]{1,0:T(8,128)S(1)}) custom-call(bf16[8192,256]{1,0:T(8,128)(2,1)} %all-gather.3.cloned.1.call-done.y_ref.src_ref, bf16[1536,256]{1,0:T(8,128)(2,1)S(1)} %copy-done.3, f32[8192,1]{1,0:T(8,128)} %copy.13.top_ref, bf16[64,8192]{1,0:T(8,128)(2,1)S(1)} %divide_convert_fusion.1.weight_ref), custom_call_target="tpu_custom_call" | custom-call | flops 8053063680 | bytes 25165824 | tf_op jit(solution)/shard_map/build_trans/pallas_call | solution.py:146
  225.3 1.4 collective-permute-start.9
  226.8 0.9 log_add_fusion
  227.7 1.5 collective-permute-start.10
  229.3 1.7 fusion
  231.5 1.0 collective-permute-done.6
  232.4 1.8 collective-permute-start.7
  234.3 1.7 collective-permute-done.7
  236.0 4.4 %collective-permute-start.8 = (f32[64]{0:T(128)S(1)}, f32[64]{0:T(128)S(1)}, u32[]{:S(2)}, u32[]{:S(2)}) collective-permute-start(f32[64]{0:T(128)S(1)} %add.86), channel_id=1, source_target_pairs={{0,4},{1,5},{2,6},{3,7},{4,0},{5,1},{6,2},{7,3},{8,12},{9,13},{10,... | collective-permute-start | bytes 776 | tf_op jit(solution)/shard_map/ppermute | solution.py:216
  240.4 1.5 collective-permute-done.8
  241.9 11.5 %collective-permute-done.10 = f32[64,1536]{1,0:T(8,128)S(1)} collective-permute-done((f32[64,1536]{1,0:T(8,128)S(1)}, f32[64,1536]{1,0:T(8,128)S(1)}, u32[]{:S(2)}, u32[]{:S(2)}) %collective-permute-start.10) | collective-permute-done | bytes 393248 | tf_op jit(solution)/shard_map/ppermute | solution.py:266
  253.5 1.3 collective-permute-start.14
  254.9 3.6 collective-permute-start.12
  258.5 1.4 collective-permute-start.13
  260.0 7.5 %collective-permute-done.12 = f32[64]{0:T(128)S(1)} collective-permute-done((f32[64]{0:T(128)S(1)}, f32[64]{0:T(128)S(1)}, u32[]{:S(2)}, u32[]{:S(2)}) %collective-permute-start.12) | collective-permute-done | bytes 288 | tf_op jit(solution)/shard_map/ppermute | solution.py:216
  267.8 1.3 collective-permute-start.15
  269.1 2.0 collective-permute-start.16
  271.1 3.1 collective-permute-done.15
  274.2 1.3 collective-permute-done.16
  275.6 5.5 %collective-permute-start.17 = (bf16[64,2048]{1,0:T(8,128)(2,1)S(1)}, bf16[64,2048]{1,0:T(8,128)(2,1)S(1)}, u32[]{:S(2)}, u32[]{:S(2)}) collective-permute-start(bf16[64,2048]{1,0:T(8,128)(2,1)S(1)} %get-tuple-element.42), channel_id=1, source_target_pairs={{0,4},{1,5},{2,6},{3,7},{10,14},{11,15},{8,12},{9,13},{20,16},{21,... | collective-permute-start | bytes 786440 | tf_op jit(solution)/shard_map/ppermute | solution.py:312
  281.1 2.0 collective-permute-start.18
  283.1 2.2 collective-permute-done.17
  285.2 1.3 collective-permute-done.18
  287.4 2.1 collective-permute-done.19
  289.9 24.1 %advance.1 = f32[64,4096]{1,0:T(8,128)} custom-call(bf16[64,8192]{1,0:T(8,128)(2,1)S(1)} %divide_convert_fusion.weight_ref, bf16[8192,2560]{1,0:T(8,128)(2,1)} %get-tuple-element.38.refs_0_, bf16[8192,1536]{1,0:T(8,128)(2,1)} %get-tuple-element.39.refs_1_), custom_call_target="tpu_custom_call" | custom-call | flops 4294967296 | bytes 67108864 | tf_op jit(solution)/shard_map/advance/pallas_call | solution.py:193
  314.0 1.4 multiply_reduce_fusion
  316.3 1.0 collective-permute-done.20
  317.3 3.5 collective-permute-start.21
  320.9 1.5 collective-permute-done.21
  322.4 3.5 collective-permute-done.22
  325.9 2.3 collective-permute-start.23
  328.2 1.5 collective-permute-done.23
  329.8 5.1 %collective-permute-done.24 = f32[64]{0:T(128)S(1)} collective-permute-done((f32[64]{0:T(128)S(1)}, f32[64]{0:T(128)S(1)}, u32[]{:S(2)}, u32[]{:S(2)}) %collective-permute-start.24) | collective-permute-done | bytes 288 | tf_op jit(solution)/shard_map/ppermute | solution.py:216
  335.3 35.6 %all-reduce.2.cloned.1.call-done = f32[64,4096]{1,0:T(8,128)} async-done(((f32[64,4096]{1,0:T(8,128)}), f32[64,4096]{1,0:T(8,128)}) %all-reduce.2.cloned.1.call-update) | async-done | bytes 1048592 | tf_op jit(solution)/shard_map/psum | solution.py:402
  371.0 2.4 multiply_divide_fusion
  (65 shorter events, 6.7 us)
Async XLA Ops:
  7.2 122.6 %all-gather.3.cloned.1.call-start = ((), (), s32[]{:S(2)}) async-start(), calls=%async_computation | async-start | bytes 4718592 | tf_op jit(solution)/shard_map/all_gather | solution.py:341
  8.7 6.2 %copy-start.1 = (bf16[4096,256]{1,0:T(8,128)(2,1)S(1)}, bf16[4096,256]{1,0:T(8,128)(2,1)}, u32[]{:S(2)}) copy-start(bf16[4096,256]{1,0:T(8,128)(2,1)} %y_ref.1) | copy-start | bytes 6291460
  11.8 114.9 %copy-start = (bf16[4096,256]{1,0:T(8,128)(2,1)S(1)}, bf16[4096,256]{1,0:T(8,128)(2,1)}, u32[]{:S(2)}) copy-start(bf16[4096,256]{1,0:T(8,128)(2,1)} %x_ref.2) | copy-start | bytes 6291460
  11.8 115.9 %collective-permute-start.1 = (bf16[128,256]{1,0:T(8,128)(2,1)S(1)}, bf16[128,256]{1,0:T(8,128)(2,1)S(1)}, u32[]{:S(2)}, u32[]{:S(2)}) collective-permute-start(bf16[128,256]{1,0:T(8,128)(2,1)S(1)} %fusion.3), channel_id=1, source_target_pairs={{0,8},{8,0},{16,24},{24,16},{1,9},{9,1},{17,25},{25,17},{2,10},{10... | collective-permute-start | bytes 196616 | tf_op jit(solution)/shard_map/ppermute | solution.py:216
  14.8 2.2 copy-start.4
  95.1 131.6 %collective-permute-start.3 = (f32[2,1,4096]{2,1,0:T(1,128)S(1)}, f32[2,1,4096]{2,1,0:T(1,128)}, u32[]{:S(2)}, u32[]{:S(2)}) collective-permute-start(f32[2,1,4096]{2,1,0:T(1,128)S(1)} %pad_maximum_fusion.2), channel_id=1, source_target_pairs={{0,8},{8,0},{16,24},{24,16},{1,9},{9,1},{17,25},{25,17},{2,10},{10... | collective-permute-start | bytes 98312 | tf_op jit(solution)/shard_map/ppermute | solution.py:216
  95.2 131.6 %collective-permute-start.4 = (f32[2,1,4096]{2,1,0:T(1,128)S(1)}, f32[2,1,4096]{2,1,0:T(1,128)}, u32[]{:S(2)}, u32[]{:S(2)}) collective-permute-start(f32[2,1,4096]{2,1,0:T(1,128)S(1)} %pad_maximum_fusion.2), channel_id=1, source_target_pairs={{0,16},{8,24},{16,0},{24,8},{1,17},{9,25},{17,1},{25,9},{2,18},{10... | collective-permute-start | bytes 98312 | tf_op jit(solution)/shard_map/ppermute | solution.py:216
  125.2 101.6 %collective-permute-start.5 = (f32[2,1,4096]{2,1,0:T(1,128)S(1)}, f32[2,1,4096]{2,1,0:T(1,128)}, u32[]{:S(2)}, u32[]{:S(2)}) collective-permute-start(f32[2,1,4096]{2,1,0:T(1,128)S(1)} %pad_maximum_fusion.2), channel_id=1, source_target_pairs={{0,24},{8,16},{16,8},{24,0},{1,25},{9,17},{17,9},{25,1},{2,26},{10... | collective-permute-start | bytes 98312 | tf_op jit(solution)/shard_map/ppermute | solution.py:216
  127.7 101.6 %collective-permute-start.2 = (bf16[128,256]{1,0:T(8,128)(2,1)S(1)}, bf16[128,256]{1,0:T(8,128)(2,1)}, u32[]{:S(2)}, u32[]{:S(2)}) collective-permute-start(bf16[128,256]{1,0:T(8,128)(2,1)S(1)} %add.78), channel_id=1, source_target_pairs={{0,16},{8,24},{16,0},{24,8},{1,17},{9,25},{17,1},{25,9},{2,18},{10... | collective-permute-start | bytes 196616 | tf_op jit(solution)/shard_map/ppermute | solution.py:216
  178.4 2.7 copy-start.5
  181.3 26.4 %copy-start.3 = (bf16[1536,256]{1,0:T(8,128)(2,1)S(1)}, bf16[1536,256]{1,0:T(8,128)(2,1)}, u32[]{:S(2)}) copy-start(bf16[1536,256]{1,0:T(8,128)(2,1)} %slice.56.dst_ref) | copy-start | bytes 2359300
  206.4 18.9 %collective-permute-start = (f32[64,2560]{1,0:T(8,128)S(1)}, f32[64,2560]{1,0:T(8,128)S(1)}, u32[]{:S(2)}, u32[]{:S(2)}) collective-permute-start(f32[64,2560]{1,0:T(8,128)S(1)} %get-tuple-element.23), channel_id=1, source_target_pairs={{8,0},{24,16},{9,1},{25,17},{2,10},{26,18},{3,11},{27,19},{4,12},{... | collective-permute-start | bytes 1966088 | tf_op jit(solution)/shard_map/ppermute | solution.py:266
  225.0 4.2 %copy-start.2 = (bf16[4096,256]{1,0:T(8,128)(2,1)S(1)}, bf16[4096,256]{1,0:T(8,128)(2,1)}, u32[]{:S(2)}) copy-start(bf16[4096,256]{1,0:T(8,128)(2,1)} %y_ref.1) | copy-start | bytes 6291460
  225.3 28.1 %collective-permute-start.9 = (f32[64,2560]{1,0:T(8,128)S(1)}, f32[64,2560]{1,0:T(8,128)S(1)}, u32[]{:S(2)}, u32[]{:S(2)}) collective-permute-start(f32[64,2560]{1,0:T(8,128)S(1)} %add.77), channel_id=1, source_target_pairs={{16,0},{17,1},{18,10},{19,11},{12,20},{13,21},{14,30},{15,31}} | collective-permute-start | bytes 1966088 | tf_op jit(solution)/shard_map/ppermute | solution.py:266
  227.7 25.7 %collective-permute-start.10 = (f32[64,1536]{1,0:T(8,128)S(1)}, f32[64,1536]{1,0:T(8,128)S(1)}, u32[]{:S(2)}, u32[]{:S(2)}) collective-permute-start(f32[64,1536]{1,0:T(8,128)S(1)} %get-tuple-element.28), channel_id=1, source_target_pairs={{8,0},{24,16},{9,1},{25,17},{2,10},{26,18},{3,11},{27,19},{4,12},{... | collective-permute-start | bytes 1179656 | tf_op jit(solution)/shard_map/ppermute | solution.py:266
  231.3 1.2 collective-permute-start.6
  232.4 3.5 collective-permute-start.7
  236.0 5.9 %collective-permute-start.8 = (f32[64]{0:T(128)S(1)}, f32[64]{0:T(128)S(1)}, u32[]{:S(2)}, u32[]{:S(2)}) collective-permute-start(f32[64]{0:T(128)S(1)} %add.86), channel_id=1, source_target_pairs={{0,4},{1,5},{2,6},{3,7},{4,0},{5,1},{6,2},{7,3},{8,12},{9,13},{10,... | collective-permute-start | bytes 776 | tf_op jit(solution)/shard_map/ppermute | solution.py:216
  253.5 14.0 %collective-permute-start.14 = (f32[64,1536]{1,0:T(8,128)S(1)}, f32[64,1536]{1,0:T(8,128)S(1)}, u32[]{:S(2)}, u32[]{:S(2)}) collective-permute-start(f32[64,1536]{1,0:T(8,128)S(1)} %add.89), channel_id=1, source_target_pairs={{16,0},{17,1},{18,10},{19,11},{12,20},{13,21},{14,30},{15,31}} | collective-permute-start | bytes 1179656 | tf_op jit(solution)/shard_map/ppermute | solution.py:266
  254.8 5.2 %collective-permute-start.11 = (f32[64]{0:T(128)S(1)}, f32[64]{0:T(128)S(1)}, u32[]{:S(2)}, u32[]{:S(2)}) collective-permute-start(f32[64]{0:T(128)S(1)} %add.87), channel_id=1, source_target_pairs={{0,8},{8,0},{16,24},{24,16},{1,9},{9,1},{17,25},{25,17},{2,10},{10... | collective-permute-start | bytes 776 | tf_op jit(solution)/shard_map/ppermute | solution.py:216
  254.9 12.6 %collective-permute-start.12 = (f32[64]{0:T(128)S(1)}, f32[64]{0:T(128)S(1)}, u32[]{:S(2)}, u32[]{:S(2)}) collective-permute-start(f32[64]{0:T(128)S(1)} %add.87), channel_id=1, source_target_pairs={{0,16},{8,24},{16,0},{24,8},{1,17},{9,25},{17,1},{25,9},{2,18},{10... | collective-permute-start | bytes 776 | tf_op jit(solution)/shard_map/ppermute | solution.py:216
  258.5 8.9 %collective-permute-start.13 = (f32[64]{0:T(128)S(1)}, f32[64]{0:T(128)S(1)}, u32[]{:S(2)}, u32[]{:S(2)}) collective-permute-start(f32[64]{0:T(128)S(1)} %add.87), channel_id=1, source_target_pairs={{0,24},{8,16},{16,8},{24,0},{1,25},{9,17},{17,9},{25,1},{2,26},{10... | collective-permute-start | bytes 776 | tf_op jit(solution)/shard_map/ppermute | solution.py:216
  267.8 6.4 %collective-permute-start.15 = (bf16[64,2048]{1,0:T(8,128)(2,1)S(1)}, bf16[64,2048]{1,0:T(8,128)(2,1)S(1)}, u32[]{:S(2)}, u32[]{:S(2)}) collective-permute-start(bf16[64,2048]{1,0:T(8,128)(2,1)S(1)} %get-tuple-element.45), channel_id=1, source_target_pairs={{0,2},{1,3},{10,8},{11,9},{20,22},{21,23},{30,28},{31,29}} | collective-permute-start | bytes 786440 | tf_op jit(solution)/shard_map/ppermute | solution.py:312
  269.1 6.4 %collective-permute-start.16 = (bf16[64,2048]{1,0:T(8,128)(2,1)S(1)}, bf16[64,2048]{1,0:T(8,128)(2,1)}, u32[]{:S(2)}, u32[]{:S(2)}) collective-permute-start(bf16[64,2048]{1,0:T(8,128)(2,1)S(1)} %get-tuple-element.44), channel_id=1, source_target_pairs={{0,4},{1,5},{10,14},{11,15},{20,16},{21,17},{30,26},{31,27}} | collective-permute-start | bytes 786440 | tf_op jit(solution)/shard_map/ppermute | solution.py:312
  275.6 9.6 %collective-permute-start.17 = (bf16[64,2048]{1,0:T(8,128)(2,1)S(1)}, bf16[64,2048]{1,0:T(8,128)(2,1)S(1)}, u32[]{:S(2)}, u32[]{:S(2)}) collective-permute-start(bf16[64,2048]{1,0:T(8,128)(2,1)S(1)} %get-tuple-element.42), channel_id=1, source_target_pairs={{0,4},{1,5},{2,6},{3,7},{10,14},{11,15},{8,12},{9,13},{20,16},{21,... | collective-permute-start | bytes 786440 | tf_op jit(solution)/shard_map/ppermute | solution.py:312
  281.1 5.5 %collective-permute-start.18 = (bf16[64,2048]{1,0:T(8,128)(2,1)S(1)}, bf16[64,2048]{1,0:T(8,128)(2,1)}, u32[]{:S(2)}, u32[]{:S(2)}) collective-permute-start(bf16[64,2048]{1,0:T(8,128)(2,1)S(1)} %get-tuple-element.43), channel_id=1, source_target_pairs={{0,2},{1,3},{4,6},{5,7},{10,8},{11,9},{14,12},{15,13},{20,22},{21,... | collective-permute-start | bytes 786440 | tf_op jit(solution)/shard_map/ppermute | solution.py:312
  287.4 2.1 collective-permute-start.19
  315.4 55.6 %all-reduce.2.cloned.1.call-start = ((), (), s32[]{:S(2)}) async-start(), calls=%async_computation.1 | async-start | bytes 2097152 | tf_op jit(solution)/shard_map/psum | solution.py:402
  316.1 1.2 collective-permute-start.20
  317.3 5.1 %collective-permute-start.21 = (f32[64]{0:T(128)S(1)}, f32[64]{0:T(128)S(1)}, u32[]{:S(2)}, u32[]{:S(2)}) collective-permute-start(f32[64]{0:T(128)S(1)} %add.94), channel_id=1, source_target_pairs={{0,2},{1,3},{2,0},{3,1},{4,6},{5,7},{6,4},{7,5},{8,10},{9,11},{10,... | collective-permute-start | bytes 776 | tf_op jit(solution)/shard_map/ppermute | solution.py:216
  322.4 3.5 collective-permute-start.22
  325.9 3.8 %collective-permute-start.23 = (f32[64]{0:T(128)S(1)}, f32[64]{0:T(128)S(1)}, u32[]{:S(2)}, u32[]{:S(2)}) collective-permute-start(f32[64]{0:T(128)S(1)} %add.96), channel_id=1, source_target_pairs={{0,8},{8,0},{16,24},{24,16},{1,9},{9,1},{17,25},{25,17},{2,10},{10... | collective-permute-start | bytes 776 | tf_op jit(solution)/shard_map/ppermute | solution.py:216
  329.8 5.1 %collective-permute-start.24 = (f32[64]{0:T(128)S(1)}, f32[64]{0:T(128)S(1)}, u32[]{:S(2)}, u32[]{:S(2)}) collective-permute-start(f32[64]{0:T(128)S(1)} %add.97), channel_id=1, source_target_pairs={{0,16},{8,24},{16,0},{24,8},{1,17},{9,25},{17,1},{25,9},{2,18},{10... | collective-permute-start | bytes 776 | tf_op jit(solution)/shard_map/ppermute | solution.py:216
Sparse Core Ops, SparseCore 0:
  9.9 39.5 all-gather.2
  319.2 51.7 all-reduce.1

commit v3 on v2

--- a/solution.py
+++ b/solution.py
@@ -171,30 +171,25 @@
     )(src, dst, top, weights)
 
 
-def advance_kernel(weight_ref, *refs):
-    trans_refs, out_ref = refs[:-1], refs[-1]
-
+def advance_kernel(weight_ref, trans_ref, out_ref):
     @pl.when(pl.program_id(0) == 0)
     def _():
         out_ref[...] = jnp.zeros_like(out_ref)
 
-    at = 0
-    for trans_ref in trans_refs:
-        here = slice(at, at + trans_ref.shape[1])
-        out_ref[:, here] += jnp.dot(weight_ref[...], trans_ref[...], preferred_element_type=F32)
-        at += trans_ref.shape[1]
+    out_ref[...] += jnp.dot(weight_ref[...], trans_ref[...], preferred_element_type=F32)
 
 
 def advance(weights, trans):
-    sources = trans[0].shape[0]
-    dests = sum(part.shape[1] for part in trans)
+    sources, dests = trans.shape
     batch = weights.shape[0]
-    rows = block_of(sources, 1024)
+    rows = block_of(sources, 2048)
     return pl.pallas_call(
         advance_kernel,
         grid=(sources // rows,),
-        in_specs=[pl.BlockSpec((batch, rows), lambda i: (0, i))]
-        + [pl.BlockSpec((rows, part.shape[1]), lambda i: (i, 0)) for part in trans],
+        in_specs=[
+            pl.BlockSpec((batch, rows), lambda i: (0, i)),
+            pl.BlockSpec((rows, dests), lambda i: (i, 0)),
+        ],
         out_specs=pl.BlockSpec((batch, dests), lambda i: (0, 0)),
         out_shape=jax.ShapeDtypeStruct((batch, dests), F32),
         compiler_params=params(),
@@ -204,7 +199,7 @@
             transcendentals=0,
         ),
         name="advance",
-    )(weights, *trans)
+    )(weights, trans)
 
 
 def bits_of(count):
@@ -241,6 +236,47 @@
     count = dests // unit
     first = max(1, count * 5 // 8)
     return [unit * size for size in (first, count - first) if size]
+
+
+def pair_stages():
+    odd = lax.axis_index("row") % 2 == 1
+
+    def apart(value):
+        half = value.shape[0] // 2
+        low, high = value[:half], value[half:]
+        return jnp.where(odd, high, low) + swapped(jnp.where(odd, low, high), "row", 1)
+
+    def across(value):
+        return value + swapped(value, "row", 2)
+
+    def together(value):
+        other = swapped(value, "row", 1)
+        return jnp.concatenate([jnp.where(odd, other, value), jnp.where(odd, value, other)], axis=0)
+
+    return [apart, across, together]
+
+
+def summed_rows(compute, rows, small, rounds):
+    if rows != 4:
+        pieces = [part([]) for part in compute]
+        small = small(pieces)
+        for step in sum(rounds, []):
+            small = step(small)
+        return [summed_all(part, ("row",)) for part in pieces], small
+    stages = pair_stages()
+    first = compute[0]([])
+    second, moved = lax.optimization_barrier((compute[1]([first]), stages[0](first)))
+    small = small([first, second])
+    pieces = [moved, second]
+    for k in range(1, len(stages) + 1):
+        for i in range(2):
+            if 0 <= k - i < len(stages):
+                pieces[i] = stages[k - i](pieces[i])
+        small = tied(small, pieces[1:])
+        for step in rounds[k - 1]:
+            small = step(small)
+        small, *pieces = lax.optimization_barrier((small, *pieces))
+    return pieces, small
 
 
 def root_hops(rows, cols):
@@ -398,11 +434,19 @@
     source_probs = to_sources(probs1, rows, cols)
     weights1 = (source_probs.astype(F32) / row_total).astype(BF16)
 
-    part = advance(weights1, trans)
-    sums2 = lax.psum(part, "row")
-    scale2 = summed_all(jnp.sum(part * emit[batch : 2 * batch], axis=1), ("col", "row"))
+    sums2, scale2 = summed_rows(
+        [
+            lambda others, built=built: advance(tied(weights1, others) if others else weights1, built)
+            for built in trans
+        ],
+        rows,
+        lambda pieces: sum(
+            jnp.sum(part * emit[batch : 2 * batch, at], axis=1) for part, at in zip(pieces, here)
+        ),
+        [col_rounds, [add_rows], []],
+    )
     scale2 = scale2 / states
-    final_probs = sums2 * emit[batch : 2 * batch] / scale2[:, None]
+    final_probs = jnp.concatenate(sums2, axis=1) * emit[batch : 2 * batch] / scale2[:, None]
     log_norm = jnp.log(scale1) + jnp.log(scale2)
     return (final_probs, log_norm)
 

time: 379 us -> 361 us (0.953); the launches traced: 380 us -> 354 us
  starting transfers between devices: 70.6 us -> 48.1 us
  waiting for transfers between devices: 83.1 us -> 78.7 us
    psum x1 -> x0, waiting for transfers between devices: 35.6 us -> none  [on_device(): sums2 = lax.psum(part, 'row')]
    ppermute x17 -> x24, starting transfers between devices: 54.2 us -> 31.9 us  [swapped(): return lax.ppermute(value, axis, [(i, i ^ mask) for i in range(count)])]
    ppermute x17 -> x24, waiting for transfers between devices: 26.5 us -> 48.3 us  [swapped(): return lax.ppermute(value, axis, [(i, i ^ mask) for i in range(count)])]
    ppermute x4, waiting for transfers between devices: 11.7 us -> 21.8 us  [root_hops(): lax.ppermute(value, ('row', 'col'), perm)]
    pallas_call x1 -> x2, Pallas kernels: 24.1 us -> 25.2 us  [advance(): pl.pallas_call(advance_kernel, grid=(sources // rows,), in_specs=[pl.Bloc...]
  transfers between devices with their start and end apart: 27 -> 33, of which waited for: 17 -> 20; matrix products, arithmetic and copies ran while one was open for 3% -> 3% of each run, Pallas kernels for 42% -> 48%
where the time goes in v3:
time: 361 us; the launch traced here: 354 us
  Pallas kernels  185 us (51%)
  waiting for transfers between devices  78.7 us (22%)
  starting transfers between devices  48.1 us (13%)
  between operations  14.5 us (4%)
  blocking collectives  9.68 us (3%)
  other arithmetic  7.04 us (2%)
  local copies, waits for them, and re-layouts  6.02 us (2%)
  matrix products  4.74 us (1%)
    pallas_call x2, Pallas kernels, column_stats(): pl.pallas_call(functools.partial(stats_kernel, rows=rows, sub=sub), grid=...  117 us
    ppermute x24, waiting for transfers between devices, swapped(): return lax.ppermute(value, axis, [(i, i ^ mask) for i in range(count)])  48.3 us
    pallas_call x2, Pallas kernels, build_and_advance(): pl.pallas_call(functools.partial(trans_kernel, cols=cols), grid=(sources...  42.4 us
    ppermute x24, starting transfers between devices, swapped(): return lax.ppermute(value, axis, [(i, i ^ mask) for i in range(count)])  31.9 us
    pallas_call x2, Pallas kernels, advance(): pl.pallas_call(advance_kernel, grid=(sources // rows,), in_specs=[pl.Bloc...  25.2 us
    ppermute x4, waiting for transfers between devices, root_hops(): lax.ppermute(value, ('row', 'col'), perm)  21.8 us
    ppermute x4, starting transfers between devices, sent(): return lax.ppermute(value, ('row', 'col'), perm)  10.8 us
    all_gather x1, blocking collectives, on_device(): every = lax.all_gather(stats, 'col')  9.68 us
  transfers between devices with their start and end apart: 33, of which 20 were waited for; matrix products, arithmetic and copies ran while one was open for 3% of the time, Pallas kernels for 48%

profile of v3, /device:TPU:0, one launch (start us, length us, event | category | flops | bytes accessed | tf_op | source)
XLA Modules:
  0.0 353.7 jit_solution(16090013016884517707)
XLA Ops:
  8.7 3.1 fusion.3
  11.8 3.1 collective-permute-start.1
  14.8 2.2 copy-done.4
  17.0 78.1 %vocab_stats.1 = (f32[1,4096]{1,0:T(1,128)S(1)}, f32[1,4096]{1,0:T(1,128)S(1)}) custom-call(bf16[8000,256]{1,0:T(8,128)(2,1)S(1)} %copy-done.4, bf16[4096,256]{1,0:T(8,128)(2,1)S(1)} %copy-done.1), custom_call_target="tpu_custom_call" | custom-call | flops 16777216000 | bytes 6193152 | tf_op jit(solution)/shard_map/vocab_stats/pallas_call | solution.py:92
  95.2 2.6 collective-permute-start.4
  97.9 1.7 collective-permute-start.5
  100.6 1.7 collective-permute-start.2
  102.4 39.2 %trans_stats.1 = (f32[1,8192]{1,0:T(1,128)S(1)}, f32[1,8192]{1,0:T(1,128)S(1)}) custom-call(bf16[4096,256]{1,0:T(8,128)(2,1)S(1)} %copy-done, bf16[8192,256]{1,0:T(8,128)(2,1)} %all-gather.3.cloned.1.call-done.y_ref.src_ref), custom_call_target="tpu_custom_call" | custom-call | flops 17179869184 | bytes 6291456 | tf_op jit(solution)/shard_map/trans_stats/pallas_call | solution.py:92
  141.7 9.7 %all-gather = f32[16,1,8192]{2,1,0:T(1,128)S(1)} all-gather(f32[2,1,8192]{2,1,0:T(1,128)S(1)} %pad_maximum_fusion.3), channel_id=2, replica_groups=mesh['row'=4,'col'=8] {'col'}, dimensions={0}, use_global_device_ids=true | all-gather | bytes 589824 | tf_op jit(solution)/shard_map/all_gather | solution.py:392
  152.1 2.7 copy.13.top_ref
  155.0 25.1 %build_trans.2 = (bf16[8192,2560]{1,0:T(8,128)(2,1)}, f32[64,2560]{1,0:T(8,128)S(1)}) custom-call(bf16[8192,256]{1,0:T(8,128)(2,1)} %all-gather.3.cloned.1.call-done.y_ref.src_ref, bf16[2560,256]{1,0:T(8,128)(2,1)S(1)} %slice.70.dst_ref, f32[8192,1]{1,0:T(8,128)} %copy.13.top_ref, bf16[64,8192]{1,0:T(8,128)(2,1)S(1)} %divide_convert_fusion.1.weight_ref), custom_call_target="tpu_custom_call" | custom-call | flops 13421772800 | bytes 41943040 | tf_op jit(solution)/shard_map/build_trans/pallas_call | solution.py:146
  180.0 1.3 collective-permute-start
  181.3 17.4 %build_trans.3 = (bf16[8192,1536]{1,0:T(8,128)(2,1)}, f32[64,1536]{1,0:T(8,128)S(1)}) custom-call(bf16[8192,256]{1,0:T(8,128)(2,1)} %all-gather.3.cloned.1.call-done.y_ref.src_ref, bf16[1536,256]{1,0:T(8,128)(2,1)S(1)} %copy-done.3, f32[8192,1]{1,0:T(8,128)} %copy.13.top_ref, bf16[64,8192]{1,0:T(8,128)(2,1)S(1)} %divide_convert_fusion.1.weight_ref), custom_call_target="tpu_custom_call" | custom-call | flops 8053063680 | bytes 25165824 | tf_op jit(solution)/shard_map/build_trans/pallas_call | solution.py:146
  198.7 11.1 %collective-permute-done = f32[64,2560]{1,0:T(8,128)S(1)} collective-permute-done((f32[64,2560]{1,0:T(8,128)S(1)}, f32[64,2560]{1,0:T(8,128)S(1)}, u32[]{:S(2)}, u32[]{:S(2)}) %collective-permute-start) | collective-permute-done | bytes 655392 | tf_op jit(solution)/shard_map/ppermute | solution.py:302
  209.8 1.3 collective-permute-start.9
  212.1 1.5 collective-permute-start.10
  213.6 1.7 fusion
  216.8 4.8 %collective-permute-start.7 = (f32[64]{0:T(128)S(1)}, f32[64]{0:T(128)S(1)}, u32[]{:S(2)}, u32[]{:S(2)}) collective-permute-start(f32[64]{0:T(128)S(1)} %add.104), channel_id=1, source_target_pairs={{0,2},{1,3},{2,0},{3,1},{4,6},{5,7},{6,4},{7,5},{8,10},{9,11},{10,... | collective-permute-start | bytes 776 | tf_op jit(solution)/shard_map/ppermute | solution.py:211
  221.6 1.5 collective-permute-done.7
  223.1 2.1 collective-permute-start.8
  225.2 1.5 collective-permute-done.8
  226.7 10.8 %collective-permute-done.10 = f32[64,1536]{1,0:T(8,128)S(1)} collective-permute-done((f32[64,1536]{1,0:T(8,128)S(1)}, f32[64,1536]{1,0:T(8,128)S(1)}, u32[]{:S(2)}, u32[]{:S(2)}) %collective-permute-start.10) | collective-permute-done | bytes 393248 | tf_op jit(solution)/shard_map/ppermute | solution.py:302
  237.5 1.3 collective-permute-start.14
  238.9 3.6 %collective-permute-start.12 = (f32[64]{0:T(128)S(1)}, f32[64]{0:T(128)S(1)}, u32[]{:S(2)}, u32[]{:S(2)}) collective-permute-start(f32[64]{0:T(128)S(1)} %add.106), channel_id=1, source_target_pairs={{0,16},{8,24},{16,0},{24,8},{1,17},{9,25},{17,1},{25,9},{2,18},{10... | collective-permute-start | bytes 776 | tf_op jit(solution)/shard_map/ppermute | solution.py:211
  242.5 1.4 collective-permute-start.13
  244.0 7.4 %collective-permute-done.12 = f32[64]{0:T(128)S(1)} collective-permute-done((f32[64]{0:T(128)S(1)}, f32[64]{0:T(128)S(1)}, u32[]{:S(2)}, u32[]{:S(2)}) %collective-permute-start.12) | collective-permute-done | bytes 288 | tf_op jit(solution)/shard_map/ppermute | solution.py:211
  251.8 1.3 collective-permute-start.15
  253.1 2.0 collective-permute-start.16
  255.1 3.1 collective-permute-done.15
  258.2 1.3 collective-permute-done.16
  259.6 5.5 %collective-permute-start.17 = (bf16[64,2048]{1,0:T(8,128)(2,1)S(1)}, bf16[64,2048]{1,0:T(8,128)(2,1)S(1)}, u32[]{:S(2)}, u32[]{:S(2)}) collective-permute-start(bf16[64,2048]{1,0:T(8,128)(2,1)S(1)} %get-tuple-element.72), channel_id=1, source_target_pairs={{0,4},{1,5},{2,6},{3,7},{10,14},{11,15},{8,12},{9,13},{20,16},{21,... | collective-permute-start | bytes 786440 | tf_op jit(solution)/shard_map/ppermute | solution.py:348
  265.0 2.0 collective-permute-start.18
  267.0 2.2 collective-permute-done.17
  269.2 1.3 collective-permute-done.18
  271.4 2.1 collective-permute-done.19
  273.8 15.1 %advance.2 = f32[64,2560]{1,0:T(8,128)S(1)} custom-call(bf16[64,8192]{1,0:T(8,128)(2,1)S(1)} %divide_convert_fusion.weight_ref, bf16[8192,2560]{1,0:T(8,128)(2,1)} %get-tuple-element.53.trans_ref), custom_call_target="tpu_custom_call" | custom-call | flops 2684354560 | bytes 41943040 | tf_op jit(solution)/shard_map/advance/pallas_call | solution.py:186
  289.0 3.9 %collective-permute-start.20 = (f32[32,2560]{1,0:T(8,128)S(1)}, f32[32,2560]{1,0:T(8,128)S(1)}, u32[]{:S(2)}, u32[]{:S(2)}) collective-permute-start(f32[32,2560]{1,0:T(8,128)S(1)} %slice_select_fusion), channel_id=1, source_target_pairs={{0,8},{8,0},{16,24},{24,16},{1,9},{9,1},{17,25},{25,17},{2,10},{10... | collective-permute-start | bytes 983048 | tf_op jit(solution)/shard_map/ppermute | solution.py:211
  292.9 10.1 %advance.3 = f32[64,1536]{1,0:T(8,128)S(1)} custom-call(bf16[64,8192]{1,0:T(8,128)(2,1)S(1)} %divide_convert_fusion.weight_ref, bf16[8192,1536]{1,0:T(8,128)(2,1)} %get-tuple-element.55.trans_ref), custom_call_target="tpu_custom_call" | custom-call | flops 1610612736 | bytes 25165824 | tf_op jit(solution)/shard_map/advance/pallas_call | solution.py:186
  303.6 7.5 %collective-permute-done.21 = f32[32,1536]{1,0:T(8,128)S(1)} collective-permute-done((f32[32,1536]{1,0:T(8,128)S(1)}, f32[32,1536]{1,0:T(8,128)S(1)}, u32[]{:S(2)}, u32[]{:S(2)}) %collective-permute-start.21) | collective-permute-done | bytes 196640 | tf_op jit(solution)/shard_map/ppermute | solution.py:211
  312.3 3.5 %collective-permute-done.23 = f32[64]{0:T(128)S(1)} collective-permute-done((f32[64]{0:T(128)S(1)}, f32[64]{0:T(128)S(1)}, u32[]{:S(2)}, u32[]{:S(2)}) %collective-permute-start.23) | collective-permute-done | bytes 288 | tf_op jit(solution)/shard_map/ppermute | solution.py:211
  315.8 3.5 %collective-permute-done.24 = f32[64]{0:T(128)S(1)} collective-permute-done((f32[64]{0:T(128)S(1)}, f32[64]{0:T(128)S(1)}, u32[]{:S(2)}, u32[]{:S(2)}) %collective-permute-start.24) | collective-permute-done | bytes 288 | tf_op jit(solution)/shard_map/ppermute | solution.py:211
  319.4 1.5 collective-permute-done.25
  321.0 1.9 collective-permute-start.30
  322.9 7.8 %collective-permute-done.26 = f32[32,1536]{1,0:T(8,128)S(1)} collective-permute-done((f32[32,1536]{1,0:T(8,128)S(1)}, f32[32,1536]{1,0:T(8,128)S(1)}, u32[]{:S(2)}, u32[]{:S(2)}) %collective-permute-start.26) | collective-permute-done | bytes 196640 | tf_op jit(solution)/shard_map/ppermute | solution.py:211
  330.9 3.0 collective-permute-start.28
  333.9 1.4 collective-permute-start.29
  335.4 3.8 %collective-permute-done.29 = f32[64]{0:T(128)S(1)} collective-permute-done((f32[64]{0:T(128)S(1)}, f32[64]{0:T(128)S(1)}, u32[]{:S(2)}, u32[]{:S(2)}) %collective-permute-start.29) | collective-permute-done | bytes 288 | tf_op jit(solution)/shard_map/ppermute | solution.py:211
  339.4 5.7 %collective-permute-done.31 = f32[32,1536]{1,0:T(8,128)S(1)} collective-permute-done((f32[32,1536]{1,0:T(8,128)S(1)}, f32[32,1536]{1,0:T(8,128)S(1)}, u32[]{:S(2)}, u32[]{:S(2)}) %collective-permute-start.31) | collective-permute-done | bytes 196640 | tf_op jit(solution)/shard_map/ppermute | solution.py:211
  (89 shorter events, 12.0 us)
Async XLA Ops:
  7.2 95.2 %all-gather.3.cloned.1.call-start = ((), (), s32[]{:S(2)}) async-start(), calls=%async_computation | async-start | bytes 4718592 | tf_op jit(solution)/shard_map/all_gather | solution.py:377
  8.7 6.2 %copy-start.1 = (bf16[4096,256]{1,0:T(8,128)(2,1)S(1)}, bf16[4096,256]{1,0:T(8,128)(2,1)}, u32[]{:S(2)}) copy-start(bf16[4096,256]{1,0:T(8,128)(2,1)} %y_ref.1) | copy-start | bytes 6291460
  11.8 87.9 %copy-start = (bf16[4096,256]{1,0:T(8,128)(2,1)S(1)}, bf16[4096,256]{1,0:T(8,128)(2,1)}, u32[]{:S(2)}) copy-start(bf16[4096,256]{1,0:T(8,128)(2,1)} %x_ref.2) | copy-start | bytes 6291460
  11.8 88.9 %collective-permute-start.1 = (bf16[128,256]{1,0:T(8,128)(2,1)S(1)}, bf16[128,256]{1,0:T(8,128)(2,1)S(1)}, u32[]{:S(2)}, u32[]{:S(2)}) collective-permute-start(bf16[128,256]{1,0:T(8,128)(2,1)S(1)} %fusion.3), channel_id=1, source_target_pairs={{0,8},{8,0},{16,24},{24,16},{1,9},{9,1},{17,25},{25,17},{2,10},{10... | collective-permute-start | bytes 196616 | tf_op jit(solution)/shard_map/ppermute | solution.py:211
  14.8 2.2 copy-start.4
  95.1 116.0 %collective-permute-start.3 = (f32[2,1,4096]{2,1,0:T(1,128)S(1)}, f32[2,1,4096]{2,1,0:T(1,128)}, u32[]{:S(2)}, u32[]{:S(2)}) collective-permute-start(f32[2,1,4096]{2,1,0:T(1,128)S(1)} %pad_maximum_fusion.4), channel_id=1, source_target_pairs={{0,8},{8,0},{16,24},{24,16},{1,9},{9,1},{17,25},{25,17},{2,10},{10... | collective-permute-start | bytes 98312 | tf_op jit(solution)/shard_map/ppermute | solution.py:211
  95.2 115.9 %collective-permute-start.4 = (f32[2,1,4096]{2,1,0:T(1,128)S(1)}, f32[2,1,4096]{2,1,0:T(1,128)}, u32[]{:S(2)}, u32[]{:S(2)}) collective-permute-start(f32[2,1,4096]{2,1,0:T(1,128)S(1)} %pad_maximum_fusion.4), channel_id=1, source_target_pairs={{0,16},{8,24},{16,0},{24,8},{1,17},{9,25},{17,1},{25,9},{2,18},{10... | collective-permute-start | bytes 98312 | tf_op jit(solution)/shard_map/ppermute | solution.py:211
  97.9 113.3 %collective-permute-start.5 = (f32[2,1,4096]{2,1,0:T(1,128)S(1)}, f32[2,1,4096]{2,1,0:T(1,128)}, u32[]{:S(2)}, u32[]{:S(2)}) collective-permute-start(f32[2,1,4096]{2,1,0:T(1,128)S(1)} %pad_maximum_fusion.4), channel_id=1, source_target_pairs={{0,24},{8,16},{16,8},{24,0},{1,25},{9,17},{17,9},{25,1},{2,26},{10... | collective-permute-start | bytes 98312 | tf_op jit(solution)/shard_map/ppermute | solution.py:211
  100.6 113.0 %collective-permute-start.2 = (bf16[128,256]{1,0:T(8,128)(2,1)S(1)}, bf16[128,256]{1,0:T(8,128)(2,1)}, u32[]{:S(2)}, u32[]{:S(2)}) collective-permute-start(bf16[128,256]{1,0:T(8,128)(2,1)S(1)} %add.97), channel_id=1, source_target_pairs={{0,16},{8,24},{16,0},{24,8},{1,17},{9,25},{17,1},{25,9},{2,18},{10... | collective-permute-start | bytes 196616 | tf_op jit(solution)/shard_map/ppermute | solution.py:211
  152.1 2.7 copy-start.5
  155.0 26.4 %copy-start.3 = (bf16[1536,256]{1,0:T(8,128)(2,1)S(1)}, bf16[1536,256]{1,0:T(8,128)(2,1)}, u32[]{:S(2)}) copy-start(bf16[1536,256]{1,0:T(8,128)(2,1)} %slice.73.dst_ref) | copy-start | bytes 2359300
  180.0 29.7 %collective-permute-start = (f32[64,2560]{1,0:T(8,128)S(1)}, f32[64,2560]{1,0:T(8,128)S(1)}, u32[]{:S(2)}, u32[]{:S(2)}) collective-permute-start(f32[64,2560]{1,0:T(8,128)S(1)} %get-tuple-element.38), channel_id=1, source_target_pairs={{8,0},{24,16},{9,1},{25,17},{2,10},{26,18},{3,11},{27,19},{4,12},{... | collective-permute-start | bytes 1966088 | tf_op jit(solution)/shard_map/ppermute | solution.py:302
  198.7 14.9 %copy-start.2 = (bf16[4096,256]{1,0:T(8,128)(2,1)S(1)}, bf16[4096,256]{1,0:T(8,128)(2,1)}, u32[]{:S(2)}) copy-start(bf16[4096,256]{1,0:T(8,128)(2,1)} %y_ref.1) | copy-start | bytes 6291460
  209.8 27.6 %collective-permute-start.9 = (f32[64,2560]{1,0:T(8,128)S(1)}, f32[64,2560]{1,0:T(8,128)S(1)}, u32[]{:S(2)}, u32[]{:S(2)}) collective-permute-start(f32[64,2560]{1,0:T(8,128)S(1)} %add.96), channel_id=1, source_target_pairs={{16,0},{17,1},{18,10},{19,11},{12,20},{13,21},{14,30},{15,31}} | collective-permute-start | bytes 1966088 | tf_op jit(solution)/shard_map/ppermute | solution.py:302
  212.1 25.4 %collective-permute-start.10 = (f32[64,1536]{1,0:T(8,128)S(1)}, f32[64,1536]{1,0:T(8,128)S(1)}, u32[]{:S(2)}, u32[]{:S(2)}) collective-permute-start(f32[64,1536]{1,0:T(8,128)S(1)} %get-tuple-element.43), channel_id=1, source_target_pairs={{8,0},{24,16},{9,1},{25,17},{2,10},{26,18},{3,11},{27,19},{4,12},{... | collective-permute-start | bytes 1179656 | tf_op jit(solution)/shard_map/ppermute | solution.py:302
  215.6 1.2 collective-permute-start.6
  216.8 6.3 %collective-permute-start.7 = (f32[64]{0:T(128)S(1)}, f32[64]{0:T(128)S(1)}, u32[]{:S(2)}, u32[]{:S(2)}) collective-permute-start(f32[64]{0:T(128)S(1)} %add.104), channel_id=1, source_target_pairs={{0,2},{1,3},{2,0},{3,1},{4,6},{5,7},{6,4},{7,5},{8,10},{9,11},{10,... | collective-permute-start | bytes 776 | tf_op jit(solution)/shard_map/ppermute | solution.py:211
  223.1 3.6 %collective-permute-start.8 = (f32[64]{0:T(128)S(1)}, f32[64]{0:T(128)S(1)}, u32[]{:S(2)}, u32[]{:S(2)}) collective-permute-start(f32[64]{0:T(128)S(1)} %add.105), channel_id=1, source_target_pairs={{0,4},{1,5},{2,6},{3,7},{4,0},{5,1},{6,2},{7,3},{8,12},{9,13},{10,... | collective-permute-start | bytes 776 | tf_op jit(solution)/shard_map/ppermute | solution.py:211
  237.5 13.9 %collective-permute-start.14 = (f32[64,1536]{1,0:T(8,128)S(1)}, f32[64,1536]{1,0:T(8,128)S(1)}, u32[]{:S(2)}, u32[]{:S(2)}) collective-permute-start(f32[64,1536]{1,0:T(8,128)S(1)} %add.108), channel_id=1, source_target_pairs={{16,0},{17,1},{18,10},{19,11},{12,20},{13,21},{14,30},{15,31}} | collective-permute-start | bytes 1179656 | tf_op jit(solution)/shard_map/ppermute | solution.py:302
  238.8 5.2 %collective-permute-start.11 = (f32[64]{0:T(128)S(1)}, f32[64]{0:T(128)S(1)}, u32[]{:S(2)}, u32[]{:S(2)}) collective-permute-start(f32[64]{0:T(128)S(1)} %add.106), channel_id=1, source_target_pairs={{0,8},{8,0},{16,24},{24,16},{1,9},{9,1},{17,25},{25,17},{2,10},{10... | collective-permute-start | bytes 776 | tf_op jit(solution)/shard_map/ppermute | solution.py:211
  238.9 12.5 %collective-permute-start.12 = (f32[64]{0:T(128)S(1)}, f32[64]{0:T(128)S(1)}, u32[]{:S(2)}, u32[]{:S(2)}) collective-permute-start(f32[64]{0:T(128)S(1)} %add.106), channel_id=1, source_target_pairs={{0,16},{8,24},{16,0},{24,8},{1,17},{9,25},{17,1},{25,9},{2,18},{10... | collective-permute-start | bytes 776 | tf_op jit(solution)/shard_map/ppermute | solution.py:211
  242.5 8.9 %collective-permute-start.13 = (f32[64]{0:T(128)S(1)}, f32[64]{0:T(128)S(1)}, u32[]{:S(2)}, u32[]{:S(2)}) collective-permute-start(f32[64]{0:T(128)S(1)} %add.106), channel_id=1, source_target_pairs={{0,24},{8,16},{16,8},{24,0},{1,25},{9,17},{17,9},{25,1},{2,26},{10... | collective-permute-start | bytes 776 | tf_op jit(solution)/shard_map/ppermute | solution.py:211
  251.8 6.4 %collective-permute-start.15 = (bf16[64,2048]{1,0:T(8,128)(2,1)S(1)}, bf16[64,2048]{1,0:T(8,128)(2,1)S(1)}, u32[]{:S(2)}, u32[]{:S(2)}) collective-permute-start(bf16[64,2048]{1,0:T(8,128)(2,1)S(1)} %get-tuple-element.75), channel_id=1, source_target_pairs={{0,2},{1,3},{10,8},{11,9},{20,22},{21,23},{30,28},{31,29}} | collective-permute-start | bytes 786440 | tf_op jit(solution)/shard_map/ppermute | solution.py:348
  253.1 6.4 %collective-permute-start.16 = (bf16[64,2048]{1,0:T(8,128)(2,1)S(1)}, bf16[64,2048]{1,0:T(8,128)(2,1)}, u32[]{:S(2)}, u32[]{:S(2)}) collective-permute-start(bf16[64,2048]{1,0:T(8,128)(2,1)S(1)} %get-tuple-element.74), channel_id=1, source_target_pairs={{0,4},{1,5},{10,14},{11,15},{20,16},{21,17},{30,26},{31,27}} | collective-permute-start | bytes 786440 | tf_op jit(solution)/shard_map/ppermute | solution.py:348
  259.6 9.6 %collective-permute-start.17 = (bf16[64,2048]{1,0:T(8,128)(2,1)S(1)}, bf16[64,2048]{1,0:T(8,128)(2,1)S(1)}, u32[]{:S(2)}, u32[]{:S(2)}) collective-permute-start(bf16[64,2048]{1,0:T(8,128)(2,1)S(1)} %get-tuple-element.72), channel_id=1, source_target_pairs={{0,4},{1,5},{2,6},{3,7},{10,14},{11,15},{8,12},{9,13},{20,16},{21,... | collective-permute-start | bytes 786440 | tf_op jit(solution)/shard_map/ppermute | solution.py:348
  265.0 5.5 %collective-permute-start.18 = (bf16[64,2048]{1,0:T(8,128)(2,1)S(1)}, bf16[64,2048]{1,0:T(8,128)(2,1)}, u32[]{:S(2)}, u32[]{:S(2)}) collective-permute-start(bf16[64,2048]{1,0:T(8,128)(2,1)S(1)} %get-tuple-element.73), channel_id=1, source_target_pairs={{0,2},{1,3},{4,6},{5,7},{10,8},{11,9},{14,12},{15,13},{20,22},{21,... | collective-permute-start | bytes 786440 | tf_op jit(solution)/shard_map/ppermute | solution.py:348
  271.4 2.1 collective-permute-start.19
  289.0 14.0 %collective-permute-start.20 = (f32[32,2560]{1,0:T(8,128)S(1)}, f32[32,2560]{1,0:T(8,128)S(1)}, u32[]{:S(2)}, u32[]{:S(2)}) collective-permute-start(f32[32,2560]{1,0:T(8,128)S(1)} %slice_select_fusion), channel_id=1, source_target_pairs={{0,8},{8,0},{16,24},{24,16},{1,9},{9,1},{17,25},{25,17},{2,10},{10... | collective-permute-start | bytes 983048 | tf_op jit(solution)/shard_map/ppermute | solution.py:211
  303.1 7.9 %collective-permute-start.21 = (f32[32,1536]{1,0:T(8,128)S(1)}, f32[32,1536]{1,0:T(8,128)S(1)}, u32[]{:S(2)}, u32[]{:S(2)}) collective-permute-start(f32[32,1536]{1,0:T(8,128)S(1)} %slice_select_fusion.1), channel_id=1, source_target_pairs={{0,8},{8,0},{16,24},{24,16},{1,9},{9,1},{17,25},{25,17},{2,10},{10... | collective-permute-start | bytes 589832 | tf_op jit(solution)/shard_map/ppermute | solution.py:211
  303.4 17.5 %collective-permute-start.25 = (f32[32,2560]{1,0:T(8,128)S(1)}, f32[32,2560]{1,0:T(8,128)S(1)}, u32[]{:S(2)}, u32[]{:S(2)}) collective-permute-start(f32[32,2560]{1,0:T(8,128)S(1)} %select_add_fusion), channel_id=1, source_target_pairs={{0,16},{8,24},{16,0},{24,8},{1,17},{9,25},{17,1},{25,9},{2,18},{10... | collective-permute-start | bytes 983048 | tf_op jit(solution)/shard_map/ppermute | solution.py:211
  311.1 1.2 collective-permute-start.22
  312.3 3.5 %collective-permute-start.23 = (f32[64]{0:T(128)S(1)}, f32[64]{0:T(128)S(1)}, u32[]{:S(2)}, u32[]{:S(2)}) collective-permute-start(f32[64]{0:T(128)S(1)} %add.117), channel_id=1, source_target_pairs={{0,2},{1,3},{2,0},{3,1},{4,6},{5,7},{6,4},{7,5},{8,10},{9,11},{10,... | collective-permute-start | bytes 776 | tf_op jit(solution)/shard_map/ppermute | solution.py:211
  315.8 3.5 %collective-permute-start.24 = (f32[64]{0:T(128)S(1)}, f32[64]{0:T(128)S(1)}, u32[]{:S(2)}, u32[]{:S(2)}) collective-permute-start(f32[64]{0:T(128)S(1)} %add.118), channel_id=1, source_target_pairs={{0,4},{1,5},{2,6},{3,7},{4,0},{5,1},{6,2},{7,3},{8,12},{9,13},{10,... | collective-permute-start | bytes 776 | tf_op jit(solution)/shard_map/ppermute | solution.py:211
  320.9 9.8 %collective-permute-start.26 = (f32[32,1536]{1,0:T(8,128)S(1)}, f32[32,1536]{1,0:T(8,128)S(1)}, u32[]{:S(2)}, u32[]{:S(2)}) collective-permute-start(f32[32,1536]{1,0:T(8,128)S(1)} %select_add_fusion.1), channel_id=1, source_target_pairs={{0,16},{8,24},{16,0},{24,8},{1,17},{9,25},{17,1},{25,9},{2,18},{10... | collective-permute-start | bytes 589832 | tf_op jit(solution)/shard_map/ppermute | solution.py:211
  321.0 18.2 %collective-permute-start.30 = (f32[32,2560]{1,0:T(8,128)S(1)}, f32[32,2560]{1,0:T(8,128)S(1)}, u32[]{:S(2)}, u32[]{:S(2)}) collective-permute-start(f32[32,2560]{1,0:T(8,128)S(1)} %add.120), channel_id=1, source_target_pairs={{0,8},{8,0},{16,24},{24,16},{1,9},{9,1},{17,25},{25,17},{2,10},{10... | collective-permute-start | bytes 983048 | tf_op jit(solution)/shard_map/ppermute | solution.py:211
  330.8 4.5 %collective-permute-start.27 = (f32[64]{0:T(128)S(1)}, f32[64]{0:T(128)S(1)}, u32[]{:S(2)}, u32[]{:S(2)}) collective-permute-start(f32[64]{0:T(128)S(1)} %add.119), channel_id=1, source_target_pairs={{0,8},{8,0},{16,24},{24,16},{1,9},{9,1},{17,25},{25,17},{2,10},{10... | collective-permute-start | bytes 776 | tf_op jit(solution)/shard_map/ppermute | solution.py:211
  330.9 4.5 %collective-permute-start.28 = (f32[64]{0:T(128)S(1)}, f32[64]{0:T(128)S(1)}, u32[]{:S(2)}, u32[]{:S(2)}) collective-permute-start(f32[64]{0:T(128)S(1)} %add.119), channel_id=1, source_target_pairs={{0,16},{8,24},{16,0},{24,8},{1,17},{9,25},{17,1},{25,9},{2,18},{10... | collective-permute-start | bytes 776 | tf_op jit(solution)/shard_map/ppermute | solution.py:211
  333.9 5.3 %collective-permute-start.29 = (f32[64]{0:T(128)S(1)}, f32[64]{0:T(128)S(1)}, u32[]{:S(2)}, u32[]{:S(2)}) collective-permute-start(f32[64]{0:T(128)S(1)} %add.119), channel_id=1, source_target_pairs={{0,24},{8,16},{16,8},{24,0},{1,25},{9,17},{17,9},{25,1},{2,26},{10... | collective-permute-start | bytes 776 | tf_op jit(solution)/shard_map/ppermute | solution.py:211
  339.3 5.7 %collective-permute-start.31 = (f32[32,1536]{1,0:T(8,128)S(1)}, f32[32,1536]{1,0:T(8,128)S(1)}, u32[]{:S(2)}, u32[]{:S(2)}) collective-permute-start(f32[32,1536]{1,0:T(8,128)S(1)} %add.121), channel_id=1, source_target_pairs={{0,8},{8,0},{16,24},{24,16},{1,9},{9,1},{17,25},{25,17},{2,10},{10... | collective-permute-start | bytes 589832 | tf_op jit(solution)/shard_map/ppermute | solution.py:211
Sparse Core Ops, SparseCore 0:
  9.9 39.4 all-gather.2

commit v4 on v3

--- a/solution.py
+++ b/solution.py
@@ -12,16 +12,15 @@
 NT = (((1,), (1,)), ((), ()))
 SPREAD = 60.0
 VMEM_LIMIT = 48 * 1024 * 1024
+SMALL_LIMIT = 40 * 1024 * 1024
 
 
 def block_of(count, most):
     return max(size for size in range(16, most + 1, 16) if count % size == 0)
 
 
-def params():
-    return pltpu.CompilerParams(
-        vmem_limit_bytes=VMEM_LIMIT, dimension_semantics=("arbitrary",)
-    )
+def params(limit=VMEM_LIMIT):
+    return pltpu.CompilerParams(vmem_limit_bytes=limit, dimension_semantics=("arbitrary",))
 
 
 def logits_of(rows, columns):
@@ -137,7 +136,7 @@
     advance(count - 1)
 
 
-def build_and_advance(src, dst, top, weights):
+def build_and_advance(src, dst, top, weights, limit):
     sources, depth = src.shape
     dests = dst.shape[0]
     batch = weights.shape[0]
@@ -161,7 +160,7 @@
             jax.ShapeDtypeStruct((batch, dests), F32),
         ],
         scratch_shapes=[pltpu.VMEM((rows, cols), F32)] * 2,
-        compiler_params=params(),
+        compiler_params=params(limit),
         cost_estimate=pl.CostEstimate(
             flops=2 * sources * dests * (depth + batch),
             bytes_accessed=2 * sources * dests,
@@ -272,7 +271,8 @@
         for i in range(2):
             if 0 <= k - i < len(stages):
                 pieces[i] = stages[k - i](pieces[i])
-        small = tied(small, pieces[1:])
+        if k == 1:
+            small = tied(small, pieces[1:])
         for step in rounds[k - 1]:
             small = step(small)
         small, *pieces = lax.optimization_barrier((small, *pieces))
@@ -414,7 +414,9 @@
     col_rounds = [add_over("col", mask) for mask in bits_of(cols)]
 
     def first_step(k, weights):
-        built, part = build_and_advance(src_rows, dst_emb[here[k]], top_column, weights)
+        built, part = build_and_advance(
+            src_rows, dst_emb[here[k]], top_column, weights, VMEM_LIMIT if k == 0 else SMALL_LIMIT
+        )
         trans.append(built)
         scales1.append(jnp.sum(part * emit[:batch, here[k]], axis=1))
         return part

time: 361 us -> 362 us (level); the launches traced: 354 us -> 365 us
  starting transfers between devices: 48.1 us -> 97.7 us
  waiting for transfers between devices: 78.7 us -> 52.8 us
  Pallas kernels: 185 us -> 168 us
  blocking collectives: 9.68 us -> 14.1 us
    ppermute x24, starting transfers between devices: 31.9 us -> 77.9 us  [swapped(): return lax.ppermute(value, axis, [(i, i ^ mask) for i in range(count)])]
    ppermute x4, waiting for transfers between devices: 21.8 us -> 3.92 us  [root_hops(): lax.ppermute(value, ('row', 'col'), perm)]
    pallas_call x2, Pallas kernels: 117 us -> 102 us  [column_stats(): pl.pallas_call(functools.partial(stats_kernel, rows=rows, sub=sub), grid=...]
    ppermute x24, waiting for transfers between devices: 48.3 us -> 41.9 us  [swapped(): return lax.ppermute(value, axis, [(i, i ^ mask) for i in range(count)])]
    all_gather x1, blocking collectives: 9.68 us -> 14.1 us  [on_device(): every = lax.all_gather(stats, 'col')]
    ppermute x4, starting transfers between devices: 10.8 us -> 14.4 us  [sent(): return lax.ppermute(value, ('row', 'col'), perm)]
  transfers between devices with their start and end apart: 33 -> 33, of which waited for: 20 -> 17; matrix products, arithmetic and copies ran while one was open for 3% -> 3% of each run, Pallas kernels for 48% -> 42%
where the time goes in v4:
time: 362 us; the launch traced here: 365 us
  Pallas kernels  168 us (46%)
  starting transfers between devices  97.7 us (27%)
  waiting for transfers between devices  52.8 us (15%)
  between operations  14.5 us (4%)
  blocking collectives  14.1 us (4%)
  other arithmetic  7.04 us (2%)
  local copies, waits for them, and re-layouts  6.01 us (2%)
  matrix products  4.73 us (1%)
    pallas_call x2, Pallas kernels, column_stats(): pl.pallas_call(functools.partial(stats_kernel, rows=rows, sub=sub), grid=...  102 us
    ppermute x24, starting transfers between devices, swapped(): return lax.ppermute(value, axis, [(i, i ^ mask) for i in range(count)])  77.9 us
    ppermute x24, waiting for transfers between devices, swapped(): return lax.ppermute(value, axis, [(i, i ^ mask) for i in range(count)])  41.9 us
    pallas_call x2, Pallas kernels, build_and_advance(): pl.pallas_call(functools.partial(trans_kernel, cols=cols), grid=(sources...  40.5 us
    pallas_call x2, Pallas kernels, advance(): pl.pallas_call(advance_kernel, grid=(sources // rows,), in_specs=[pl.Bloc...  25.2 us
    ppermute x4, starting transfers between devices, sent(): return lax.ppermute(value, ('row', 'col'), perm)  14.4 us
    all_gather x1, blocking collectives, on_device(): every = lax.all_gather(stats, 'col')  14.1 us
  transfers between devices with their start and end apart: 33, of which 17 were waited for; matrix products, arithmetic and copies ran while one was open for 3% of the time, Pallas kernels for 42%

profile of v4, /device:TPU:0, one launch (start us, length us, event | category | flops | bytes accessed | tf_op | source)
XLA Modules:
  0.0 364.7 jit_solution(7226223270128597256)
XLA Ops:
  8.7 3.1 fusion.3
  11.8 3.1 collective-permute-start.1
  14.8 2.2 copy-done.6
  17.0 50.8 %vocab_stats.1 = (f32[1,4096]{1,0:T(1,128)S(1)}, f32[1,4096]{1,0:T(1,128)S(1)}) custom-call(bf16[8000,256]{1,0:T(8,128)(2,1)S(1)} %copy-done.6, bf16[4096,256]{1,0:T(8,128)(2,1)S(1)} %copy-done.2), custom_call_target="tpu_custom_call" | custom-call | flops 16777216000 | bytes 6193152 | tf_op jit(solution)/shard_map/vocab_stats/pallas_call | solution.py:91
  67.9 30.5 %collective-permute-start.4 = (f32[2,1,4096]{2,1,0:T(1,128)S(1)}, f32[2,1,4096]{2,1,0:T(1,128)}, u32[]{:S(2)}, u32[]{:S(2)}) collective-permute-start(f32[2,1,4096]{2,1,0:T(1,128)S(1)} %pad_maximum_fusion.4), channel_id=1, source_target_pairs={{0,16},{8,24},{16,0},{24,8},{1,17},{9,25},{17,1},{25,9},{2,18},{10... | collective-permute-start | bytes 98312 | tf_op jit(solution)/shard_map/ppermute | solution.py:210
  99.4 1.6 collective-permute-start.2
  101.0 51.4 %trans_stats.1 = (f32[1,8192]{1,0:T(1,128)S(1)}, f32[1,8192]{1,0:T(1,128)S(1)}) custom-call(bf16[4096,256]{1,0:T(8,128)(2,1)S(1)} %copy-done.1, bf16[8192,256]{1,0:T(8,128)(2,1)} %all-gather.3.cloned.1.call-done.y_ref.src_ref), custom_call_target="tpu_custom_call" | custom-call | flops 17179869184 | bytes 6291456 | tf_op jit(solution)/shard_map/trans_stats/pallas_call | solution.py:91
  152.5 14.1 %all-gather = f32[16,1,8192]{2,1,0:T(1,128)S(1)} all-gather(f32[2,1,8192]{2,1,0:T(1,128)S(1)} %pad_maximum_fusion.3), channel_id=2, replica_groups=mesh['row'=4,'col'=8] {'col'}, dimensions={0}, use_global_device_ids=true | all-gather | bytes 589824 | tf_op jit(solution)/shard_map/all_gather | solution.py:392
  167.3 2.7 copy.13.top_ref
  170.2 25.1 %build_trans.2 = (bf16[8192,2560]{1,0:T(8,128)(2,1)}, f32[64,2560]{1,0:T(8,128)S(1)}) custom-call(bf16[8192,256]{1,0:T(8,128)(2,1)} %all-gather.3.cloned.1.call-done.y_ref.src_ref, bf16[2560,256]{1,0:T(8,128)(2,1)S(1)} %slice.70.dst_ref, f32[8192,1]{1,0:T(8,128)} %copy.13.top_ref, bf16[64,8192]{1,0:T(8,128)(2,1)S(1)} %divide_convert_fusion.1.weight_ref), custom_call_target="tpu_custom_call" | custom-call | flops 13421772800 | bytes 41943040 | tf_op jit(solution)/shard_map/build_trans/pallas_call | solution.py:145
  195.3 1.3 collective-permute-start
  196.7 15.3 %build_trans.3 = (bf16[8192,1536]{1,0:T(8,128)(2,1)}, f32[64,1536]{1,0:T(8,128)S(1)}) custom-call(bf16[8192,256]{1,0:T(8,128)(2,1)S(1)} %copy-done.5, bf16[1536,256]{1,0:T(8,128)(2,1)S(1)} %copy-done.4, f32[8192,1]{1,0:T(8,128)S(1)} %copy-done, bf16[64,8192]{1,0:T(8,128)(2,1)S(1)} %divide_convert_fusion.1.weight_ref), custom_call_target="tpu_custom_call" | custom-call | flops 8053063680 | bytes 25165824 | tf_op jit(solution)/shard_map/build_trans/pallas_call | solution.py:145
  212.0 2.2 collective-permute-done
  214.3 1.3 collective-permute-start.9
  216.5 1.5 collective-permute-start.10
  218.1 1.7 fusion
  220.1 1.1 collective-permute-done.6
  221.3 2.0 collective-permute-start.7
  223.2 1.5 collective-permute-done.7
  224.8 15.0 %collective-permute-start.8 = (f32[64]{0:T(128)S(1)}, f32[64]{0:T(128)S(1)}, u32[]{:S(2)}, u32[]{:S(2)}) collective-permute-start(f32[64]{0:T(128)S(1)} %add.105), channel_id=1, source_target_pairs={{0,4},{1,5},{2,6},{3,7},{4,0},{5,1},{6,2},{7,3},{8,12},{9,13},{10,... | collective-permute-start | bytes 776 | tf_op jit(solution)/shard_map/ppermute | solution.py:210
  239.8 1.5 collective-permute-done.8
  241.4 1.7 collective-permute-done.10
  243.1 1.3 collective-permute-start.14
  244.5 3.6 collective-permute-start.12
  248.1 1.4 collective-permute-start.13
  249.6 5.3 %collective-permute-done.12 = f32[64]{0:T(128)S(1)} collective-permute-done((f32[64]{0:T(128)S(1)}, f32[64]{0:T(128)S(1)}, u32[]{:S(2)}, u32[]{:S(2)}) %collective-permute-start.12) | collective-permute-done | bytes 288 | tf_op jit(solution)/shard_map/ppermute | solution.py:210
  255.2 1.3 collective-permute-start.15
  256.5 2.0 collective-permute-start.16
  258.5 1.8 collective-permute-done.15
  260.4 1.3 collective-permute-done.16
  261.7 5.5 %collective-permute-start.17 = (bf16[64,2048]{1,0:T(8,128)(2,1)S(1)}, bf16[64,2048]{1,0:T(8,128)(2,1)S(1)}, u32[]{:S(2)}, u32[]{:S(2)}) collective-permute-start(bf16[64,2048]{1,0:T(8,128)(2,1)S(1)} %get-tuple-element.68), channel_id=1, source_target_pairs={{0,4},{1,5},{2,6},{3,7},{10,14},{11,15},{8,12},{9,13},{20,16},{21,... | collective-permute-start | bytes 786440 | tf_op jit(solution)/shard_map/ppermute | solution.py:348
  267.2 5.6 %collective-permute-start.18 = (bf16[64,2048]{1,0:T(8,128)(2,1)S(1)}, bf16[64,2048]{1,0:T(8,128)(2,1)}, u32[]{:S(2)}, u32[]{:S(2)}) collective-permute-start(bf16[64,2048]{1,0:T(8,128)(2,1)S(1)} %get-tuple-element.69), channel_id=1, source_target_pairs={{0,2},{1,3},{4,6},{5,7},{10,8},{11,9},{14,12},{15,13},{20,22},{21,... | collective-permute-start | bytes 786440 | tf_op jit(solution)/shard_map/ppermute | solution.py:348
  272.8 3.2 collective-permute-done.18
  276.9 2.1 collective-permute-done.19
  279.3 15.1 %advance.2 = f32[64,2560]{1,0:T(8,128)S(1)} custom-call(bf16[64,8192]{1,0:T(8,128)(2,1)S(1)} %divide_convert_fusion.weight_ref, bf16[8192,2560]{1,0:T(8,128)(2,1)} %get-tuple-element.51.trans_ref), custom_call_target="tpu_custom_call" | custom-call | flops 2684354560 | bytes 41943040 | tf_op jit(solution)/shard_map/advance/pallas_call | solution.py:185
  294.5 12.2 %collective-permute-start.20 = (f32[32,2560]{1,0:T(8,128)S(1)}, f32[32,2560]{1,0:T(8,128)S(1)}, u32[]{:S(2)}, u32[]{:S(2)}) collective-permute-start(f32[32,2560]{1,0:T(8,128)S(1)} %slice_select_fusion), channel_id=1, source_target_pairs={{0,8},{8,0},{16,24},{24,16},{1,9},{9,1},{17,25},{25,17},{2,10},{10... | collective-permute-start | bytes 983048 | tf_op jit(solution)/shard_map/ppermute | solution.py:210
  306.7 10.1 %advance.3 = f32[64,1536]{1,0:T(8,128)S(1)} custom-call(bf16[64,8192]{1,0:T(8,128)(2,1)S(1)} %divide_convert_fusion.weight_ref, bf16[8192,1536]{1,0:T(8,128)(2,1)} %get-tuple-element.53.trans_ref), custom_call_target="tpu_custom_call" | custom-call | flops 1610612736 | bytes 25165824 | tf_op jit(solution)/shard_map/advance/pallas_call | solution.py:185
  317.2 1.8 collective-permute-start.25
  319.2 8.5 %collective-permute-done.21 = f32[32,1536]{1,0:T(8,128)S(1)} collective-permute-done((f32[32,1536]{1,0:T(8,128)S(1)}, f32[32,1536]{1,0:T(8,128)S(1)}, u32[]{:S(2)}, u32[]{:S(2)}) %collective-permute-start.21) | collective-permute-done | bytes 196640 | tf_op jit(solution)/shard_map/ppermute | solution.py:210
  327.8 1.1 collective-permute-done.22
  328.9 3.5 collective-permute-done.23
  333.3 2.7 collective-permute-done.24
  336.1 2.0 collective-permute-start.26
  338.2 2.4 collective-permute-start.28
  341.5 5.2 %collective-permute-done.26 = f32[64]{0:T(128)S(1)} collective-permute-done((f32[64]{0:T(128)S(1)}, f32[64]{0:T(128)S(1)}, u32[]{:S(2)}, u32[]{:S(2)}) %collective-permute-start.26) | collective-permute-done | bytes 288 | tf_op jit(solution)/shard_map/ppermute | solution.py:210
  346.7 3.5 collective-permute-done.30
  350.4 5.7 %collective-permute-done.31 = f32[32,1536]{1,0:T(8,128)S(1)} collective-permute-done((f32[32,1536]{1,0:T(8,128)S(1)}, f32[32,1536]{1,0:T(8,128)S(1)}, u32[]{:S(2)}, u32[]{:S(2)}) %collective-permute-start.31) | collective-permute-done | bytes 196640 | tf_op jit(solution)/shard_map/ppermute | solution.py:210
  356.7 1.2 fusion.4
  (93 shorter events, 10.0 us)
Async XLA Ops:
  7.2 93.9 %all-gather.3.cloned.1.call-start = ((), (), s32[]{:S(2)}) async-start(), calls=%async_computation | async-start | bytes 4718592 | tf_op jit(solution)/shard_map/all_gather | solution.py:377
  8.7 6.2 %copy-start.2 = (bf16[4096,256]{1,0:T(8,128)(2,1)S(1)}, bf16[4096,256]{1,0:T(8,128)(2,1)}, u32[]{:S(2)}) copy-start(bf16[4096,256]{1,0:T(8,128)(2,1)} %y_ref.1) | copy-start | bytes 6291460
  11.8 86.6 %copy-start.1 = (bf16[4096,256]{1,0:T(8,128)(2,1)S(1)}, bf16[4096,256]{1,0:T(8,128)(2,1)}, u32[]{:S(2)}) copy-start(bf16[4096,256]{1,0:T(8,128)(2,1)} %x_ref.2) | copy-start | bytes 6291460
  11.8 87.6 %collective-permute-start.1 = (bf16[128,256]{1,0:T(8,128)(2,1)S(1)}, bf16[128,256]{1,0:T(8,128)(2,1)S(1)}, u32[]{:S(2)}, u32[]{:S(2)}) collective-permute-start(bf16[128,256]{1,0:T(8,128)(2,1)S(1)} %fusion.3), channel_id=1, source_target_pairs={{0,8},{8,0},{16,24},{24,16},{1,9},{9,1},{17,25},{25,17},{2,10},{10... | collective-permute-start | bytes 196616 | tf_op jit(solution)/shard_map/ppermute | solution.py:210
  14.8 2.2 copy-start.6
  67.8 147.8 %collective-permute-start.3 = (f32[2,1,4096]{2,1,0:T(1,128)S(1)}, f32[2,1,4096]{2,1,0:T(1,128)}, u32[]{:S(2)}, u32[]{:S(2)}) collective-permute-start(f32[2,1,4096]{2,1,0:T(1,128)S(1)} %pad_maximum_fusion.4), channel_id=1, source_target_pairs={{0,8},{8,0},{16,24},{24,16},{1,9},{9,1},{17,25},{25,17},{2,10},{10... | collective-permute-start | bytes 98312 | tf_op jit(solution)/shard_map/ppermute | solution.py:210
  67.9 147.7 %collective-permute-start.4 = (f32[2,1,4096]{2,1,0:T(1,128)S(1)}, f32[2,1,4096]{2,1,0:T(1,128)}, u32[]{:S(2)}, u32[]{:S(2)}) collective-permute-start(f32[2,1,4096]{2,1,0:T(1,128)S(1)} %pad_maximum_fusion.4), channel_id=1, source_target_pairs={{0,16},{8,24},{16,0},{24,8},{1,17},{9,25},{17,1},{25,9},{2,18},{10... | collective-permute-start | bytes 98312 | tf_op jit(solution)/shard_map/ppermute | solution.py:210
  98.4 117.2 %collective-permute-start.5 = (f32[2,1,4096]{2,1,0:T(1,128)S(1)}, f32[2,1,4096]{2,1,0:T(1,128)}, u32[]{:S(2)}, u32[]{:S(2)}) collective-permute-start(f32[2,1,4096]{2,1,0:T(1,128)S(1)} %pad_maximum_fusion.4), channel_id=1, source_target_pairs={{0,24},{8,16},{16,8},{24,0},{1,25},{9,17},{17,9},{25,1},{2,26},{10... | collective-permute-start | bytes 98312 | tf_op jit(solution)/shard_map/ppermute | solution.py:210
  99.4 118.6 %collective-permute-start.2 = (bf16[128,256]{1,0:T(8,128)(2,1)S(1)}, bf16[128,256]{1,0:T(8,128)(2,1)}, u32[]{:S(2)}, u32[]{:S(2)}) collective-permute-start(bf16[128,256]{1,0:T(8,128)(2,1)S(1)} %add.97), channel_id=1, source_target_pairs={{0,16},{8,24},{16,0},{24,8},{1,17},{9,25},{17,1},{25,9},{2,18},{10... | collective-permute-start | bytes 196616 | tf_op jit(solution)/shard_map/ppermute | solution.py:210
  167.3 2.7 copy-start.7
  170.2 26.5 %copy-start = (f32[8192,1]{1,0:T(8,128)S(1)}, f32[8192,1]{1,0:T(8,128)}, u32[]{:S(2)}) copy-start(f32[8192,1]{1,0:T(8,128)} %copy.13.top_ref) | copy-start | bytes 98308
  170.2 26.5 %copy-start.4 = (bf16[1536,256]{1,0:T(8,128)(2,1)S(1)}, bf16[1536,256]{1,0:T(8,128)(2,1)}, u32[]{:S(2)}) copy-start(bf16[1536,256]{1,0:T(8,128)(2,1)} %slice.73.dst_ref) | copy-start | bytes 2359300
  170.2 26.5 %copy-start.5 = (bf16[8192,256]{1,0:T(8,128)(2,1)S(1)}, bf16[8192,256]{1,0:T(8,128)(2,1)}, u32[]{:S(2)}) copy-start(bf16[8192,256]{1,0:T(8,128)(2,1)} %all-gather.3.cloned.1.call-done.y_ref.src_ref) | copy-start | bytes 12582916
  195.3 18.9 %collective-permute-start = (f32[64,2560]{1,0:T(8,128)S(1)}, f32[64,2560]{1,0:T(8,128)S(1)}, u32[]{:S(2)}, u32[]{:S(2)}) collective-permute-start(f32[64,2560]{1,0:T(8,128)S(1)} %get-tuple-element.36), channel_id=1, source_target_pairs={{8,0},{24,16},{9,1},{25,17},{2,10},{26,18},{3,11},{27,19},{4,12},{... | collective-permute-start | bytes 1966088 | tf_op jit(solution)/shard_map/ppermute | solution.py:302
  212.0 6.1 %copy-start.3 = (bf16[4096,256]{1,0:T(8,128)(2,1)S(1)}, bf16[4096,256]{1,0:T(8,128)(2,1)}, u32[]{:S(2)}) copy-start(bf16[4096,256]{1,0:T(8,128)(2,1)} %y_ref.1) | copy-start | bytes 6291460
  214.3 28.8 %collective-permute-start.9 = (f32[64,2560]{1,0:T(8,128)S(1)}, f32[64,2560]{1,0:T(8,128)S(1)}, u32[]{:S(2)}, u32[]{:S(2)}) collective-permute-start(f32[64,2560]{1,0:T(8,128)S(1)} %add.96), channel_id=1, source_target_pairs={{16,0},{17,1},{18,10},{19,11},{12,20},{13,21},{14,30},{15,31}} | collective-permute-start | bytes 1966088 | tf_op jit(solution)/shard_map/ppermute | solution.py:302
  216.5 26.5 %collective-permute-start.10 = (f32[64,1536]{1,0:T(8,128)S(1)}, f32[64,1536]{1,0:T(8,128)S(1)}, u32[]{:S(2)}, u32[]{:S(2)}) collective-permute-start(f32[64,1536]{1,0:T(8,128)S(1)} %get-tuple-element.41), channel_id=1, source_target_pairs={{8,0},{24,16},{9,1},{25,17},{2,10},{26,18},{3,11},{27,19},{4,12},{... | collective-permute-start | bytes 1179656 | tf_op jit(solution)/shard_map/ppermute | solution.py:302
  220.1 1.2 collective-permute-start.6
  221.3 3.5 collective-permute-start.7
  224.8 16.6 %collective-permute-start.8 = (f32[64]{0:T(128)S(1)}, f32[64]{0:T(128)S(1)}, u32[]{:S(2)}, u32[]{:S(2)}) collective-permute-start(f32[64]{0:T(128)S(1)} %add.105), channel_id=1, source_target_pairs={{0,4},{1,5},{2,6},{3,7},{4,0},{5,1},{6,2},{7,3},{8,12},{9,13},{10,... | collective-permute-start | bytes 776 | tf_op jit(solution)/shard_map/ppermute | solution.py:210
  243.1 11.8 %collective-permute-start.14 = (f32[64,1536]{1,0:T(8,128)S(1)}, f32[64,1536]{1,0:T(8,128)S(1)}, u32[]{:S(2)}, u32[]{:S(2)}) collective-permute-start(f32[64,1536]{1,0:T(8,128)S(1)} %add.108), channel_id=1, source_target_pairs={{16,0},{17,1},{18,10},{19,11},{12,20},{13,21},{14,30},{15,31}} | collective-permute-start | bytes 1179656 | tf_op jit(solution)/shard_map/ppermute | solution.py:302
  244.4 5.2 %collective-permute-start.11 = (f32[64]{0:T(128)S(1)}, f32[64]{0:T(128)S(1)}, u32[]{:S(2)}, u32[]{:S(2)}) collective-permute-start(f32[64]{0:T(128)S(1)} %add.106), channel_id=1, source_target_pairs={{0,8},{8,0},{16,24},{24,16},{1,9},{9,1},{17,25},{25,17},{2,10},{10... | collective-permute-start | bytes 776 | tf_op jit(solution)/shard_map/ppermute | solution.py:210
  244.5 10.4 %collective-permute-start.12 = (f32[64]{0:T(128)S(1)}, f32[64]{0:T(128)S(1)}, u32[]{:S(2)}, u32[]{:S(2)}) collective-permute-start(f32[64]{0:T(128)S(1)} %add.106), channel_id=1, source_target_pairs={{0,16},{8,24},{16,0},{24,8},{1,17},{9,25},{17,1},{25,9},{2,18},{10... | collective-permute-start | bytes 776 | tf_op jit(solution)/shard_map/ppermute | solution.py:210
  248.1 6.7 %collective-permute-start.13 = (f32[64]{0:T(128)S(1)}, f32[64]{0:T(128)S(1)}, u32[]{:S(2)}, u32[]{:S(2)}) collective-permute-start(f32[64]{0:T(128)S(1)} %add.106), channel_id=1, source_target_pairs={{0,24},{8,16},{16,8},{24,0},{1,25},{9,17},{17,9},{25,1},{2,26},{10... | collective-permute-start | bytes 776 | tf_op jit(solution)/shard_map/ppermute | solution.py:210
  255.2 5.2 %collective-permute-start.15 = (bf16[64,2048]{1,0:T(8,128)(2,1)S(1)}, bf16[64,2048]{1,0:T(8,128)(2,1)S(1)}, u32[]{:S(2)}, u32[]{:S(2)}) collective-permute-start(bf16[64,2048]{1,0:T(8,128)(2,1)S(1)} %get-tuple-element.71), channel_id=1, source_target_pairs={{0,2},{1,3},{10,8},{11,9},{20,22},{21,23},{30,28},{31,29}} | collective-permute-start | bytes 786440 | tf_op jit(solution)/shard_map/ppermute | solution.py:348
  256.5 5.2 %collective-permute-start.16 = (bf16[64,2048]{1,0:T(8,128)(2,1)S(1)}, bf16[64,2048]{1,0:T(8,128)(2,1)}, u32[]{:S(2)}, u32[]{:S(2)}) collective-permute-start(bf16[64,2048]{1,0:T(8,128)(2,1)S(1)} %get-tuple-element.70), channel_id=1, source_target_pairs={{0,4},{1,5},{10,14},{11,15},{20,16},{21,17},{30,26},{31,27}} | collective-permute-start | bytes 786440 | tf_op jit(solution)/shard_map/ppermute | solution.py:348
  261.7 11.1 %collective-permute-start.17 = (bf16[64,2048]{1,0:T(8,128)(2,1)S(1)}, bf16[64,2048]{1,0:T(8,128)(2,1)S(1)}, u32[]{:S(2)}, u32[]{:S(2)}) collective-permute-start(bf16[64,2048]{1,0:T(8,128)(2,1)S(1)} %get-tuple-element.68), channel_id=1, source_target_pairs={{0,4},{1,5},{2,6},{3,7},{10,14},{11,15},{8,12},{9,13},{20,16},{21,... | collective-permute-start | bytes 786440 | tf_op jit(solution)/shard_map/ppermute | solution.py:348
  267.2 8.8 %collective-permute-start.18 = (bf16[64,2048]{1,0:T(8,128)(2,1)S(1)}, bf16[64,2048]{1,0:T(8,128)(2,1)}, u32[]{:S(2)}, u32[]{:S(2)}) collective-permute-start(bf16[64,2048]{1,0:T(8,128)(2,1)S(1)} %get-tuple-element.69), channel_id=1, source_target_pairs={{0,2},{1,3},{4,6},{5,7},{10,8},{11,9},{14,12},{15,13},{20,22},{21,... | collective-permute-start | bytes 786440 | tf_op jit(solution)/shard_map/ppermute | solution.py:348
  276.9 2.1 collective-permute-start.19
  294.5 22.3 %collective-permute-start.20 = (f32[32,2560]{1,0:T(8,128)S(1)}, f32[32,2560]{1,0:T(8,128)S(1)}, u32[]{:S(2)}, u32[]{:S(2)}) collective-permute-start(f32[32,2560]{1,0:T(8,128)S(1)} %slice_select_fusion), channel_id=1, source_target_pairs={{0,8},{8,0},{16,24},{24,16},{1,9},{9,1},{17,25},{25,17},{2,10},{10... | collective-permute-start | bytes 983048 | tf_op jit(solution)/shard_map/ppermute | solution.py:210
  316.9 10.8 %collective-permute-start.21 = (f32[32,1536]{1,0:T(8,128)S(1)}, f32[32,1536]{1,0:T(8,128)S(1)}, u32[]{:S(2)}, u32[]{:S(2)}) collective-permute-start(f32[32,1536]{1,0:T(8,128)S(1)} %slice_select_fusion.1), channel_id=1, source_target_pairs={{0,8},{8,0},{16,24},{24,16},{1,9},{9,1},{17,25},{25,17},{2,10},{10... | collective-permute-start | bytes 589832 | tf_op jit(solution)/shard_map/ppermute | solution.py:210
  317.2 18.8 %collective-permute-start.25 = (f32[32,2560]{1,0:T(8,128)S(1)}, f32[32,2560]{1,0:T(8,128)S(1)}, u32[]{:S(2)}, u32[]{:S(2)}) collective-permute-start(f32[32,2560]{1,0:T(8,128)S(1)} %select_add_fusion), channel_id=1, source_target_pairs={{0,16},{8,24},{16,0},{24,8},{1,17},{9,25},{17,1},{25,9},{2,18},{10... | collective-permute-start | bytes 983048 | tf_op jit(solution)/shard_map/ppermute | solution.py:210
  327.7 1.2 collective-permute-start.22
  328.9 3.5 collective-permute-start.23
  332.5 3.5 collective-permute-start.24
  336.1 14.2 %collective-permute-start.29 = (f32[32,2560]{1,0:T(8,128)S(1)}, f32[32,2560]{1,0:T(8,128)S(1)}, u32[]{:S(2)}, u32[]{:S(2)}) collective-permute-start(f32[32,2560]{1,0:T(8,128)S(1)} %add.120), channel_id=1, source_target_pairs={{0,8},{8,0},{16,24},{24,16},{1,9},{9,1},{17,25},{25,17},{2,10},{10... | collective-permute-start | bytes 983048 | tf_op jit(solution)/shard_map/ppermute | solution.py:210
  336.1 10.6 %collective-permute-start.26 = (f32[64]{0:T(128)S(1)}, f32[64]{0:T(128)S(1)}, u32[]{:S(2)}, u32[]{:S(2)}) collective-permute-start(f32[64]{0:T(128)S(1)} %add.119), channel_id=1, source_target_pairs={{0,8},{8,0},{16,24},{24,16},{1,9},{9,1},{17,25},{25,17},{2,10},{10... | collective-permute-start | bytes 776 | tf_op jit(solution)/shard_map/ppermute | solution.py:210
  338.2 8.6 %collective-permute-start.27 = (f32[64]{0:T(128)S(1)}, f32[64]{0:T(128)S(1)}, u32[]{:S(2)}, u32[]{:S(2)}) collective-permute-start(f32[64]{0:T(128)S(1)} %add.119), channel_id=1, source_target_pairs={{0,16},{8,24},{16,0},{24,8},{1,17},{9,25},{17,1},{25,9},{2,18},{10... | collective-permute-start | bytes 776 | tf_op jit(solution)/shard_map/ppermute | solution.py:210
  338.2 8.6 %collective-permute-start.28 = (f32[64]{0:T(128)S(1)}, f32[64]{0:T(128)S(1)}, u32[]{:S(2)}, u32[]{:S(2)}) collective-permute-start(f32[64]{0:T(128)S(1)} %add.119), channel_id=1, source_target_pairs={{0,24},{8,16},{16,8},{24,0},{1,25},{9,17},{17,9},{25,1},{2,26},{10... | collective-permute-start | bytes 776 | tf_op jit(solution)/shard_map/ppermute | solution.py:210
  340.6 9.6 %collective-permute-start.30 = (f32[32,1536]{1,0:T(8,128)S(1)}, f32[32,1536]{1,0:T(8,128)S(1)}, u32[]{:S(2)}, u32[]{:S(2)}) collective-permute-start(f32[32,1536]{1,0:T(8,128)S(1)} %select_add_fusion.1), channel_id=1, source_target_pairs={{0,16},{8,24},{16,0},{24,8},{1,17},{9,25},{17,1},{25,9},{2,18},{10... | collective-permute-start | bytes 589832 | tf_op jit(solution)/shard_map/ppermute | solution.py:210
  350.4 5.7 %collective-permute-start.31 = (f32[32,1536]{1,0:T(8,128)S(1)}, f32[32,1536]{1,0:T(8,128)S(1)}, u32[]{:S(2)}, u32[]{:S(2)}) collective-permute-start(f32[32,1536]{1,0:T(8,128)S(1)} %add.124), channel_id=1, source_target_pairs={{0,8},{8,0},{16,24},{24,16},{1,9},{9,1},{17,25},{25,17},{2,10},{10... | collective-permute-start | bytes 589832 | tf_op jit(solution)/shard_map/ppermute | solution.py:210
Sparse Core Ops, SparseCore 0:
  9.9 39.4 all-gather.2
